TPU v7x, 512 devices: a whole 4x4x16 slice. The times are simulated.
512 devices in a mesh: clip: 4 (over y), video: 32 (over z, core), audio: 4 (over x).
Axes of the slice: x: 4, y: 4, z: 16, core: 2. Of those that a mesh axis runs over, the one named last changes fastest.
Arguments:
- video_query: bfloat16 [16384, 3072], P(('clip', 'video'), 'audio'), parts along dimension 0, may hold values from -5 to 5
- video_key: bfloat16 [16384, 3072], P(('clip', 'video'), 'audio'), parts along dimension 0, may hold values from -5 to 5
- video_value: bfloat16 [16384, 3072], P(('clip', 'video'), 'audio'), parts along dimension 0, may hold values from -5 to 5
- video_cot: bfloat16 [16384, 3072], P(('clip', 'video'), 'audio'), parts along dimension 0, may hold values from -5 to 5
- audio_query: bfloat16 [8192, 3072], P(('clip', 'video'), 'audio'), parts along dimension 0, may hold values from -5 to 5
- audio_key: bfloat16 [8192, 3072], P(('clip', 'video'), 'audio'), parts along dimension 0, may hold values from -5 to 5
- audio_value: bfloat16 [8192, 3072], P(('clip', 'video'), 'audio'), parts along dimension 0, may hold values from -5 to 5
- audio_cot: bfloat16 [8192, 3072], P(('clip', 'video'), 'audio'), parts along dimension 0, may hold values from -5 to 5
- intersection: int32 [128, 2], P('clip'), parts along dimension 0, may hold values from 0 to 2048, as said below
Outputs:
- video_out: bfloat16 [16384, 3072], P(('clip', 'video'), 'audio'), parts along dimension 0
- audio_out: bfloat16 [8192, 3072], P(('clip', 'video'), 'audio'), parts along dimension 0
- video_query_grad: bfloat16 [16384, 3072], P(('clip', 'video'), 'audio'), parts along dimension 0
- video_key_grad: bfloat16 [16384, 3072], P(('clip', 'video'), 'audio'), parts along dimension 0
- video_value_grad: bfloat16 [16384, 3072], P(('clip', 'video'), 'audio'), parts along dimension 0
- audio_query_grad: bfloat16 [8192, 3072], P(('clip', 'video'), 'audio'), parts along dimension 0
- audio_key_grad: bfloat16 [8192, 3072], P(('clip', 'video'), 'audio'), parts along dimension 0
- audio_value_grad: bfloat16 [8192, 3072], P(('clip', 'video'), 'audio'), parts along dimension 0
There are 4 independent parts, one for each index of `clip`. A program takes and returns all parts, laid end to end along the dimension named above; each array names one. Nothing has to cross between parts.
Inputs may be any that keep to these rules, and one draw needn't show every extreme that they name: `intersection`: row b holds two audio row numbers: the first lies from max(0, (b - 1) * 64) to b * 64, the second from (b + 1) * 64 to min(2048, (b + 2) * 64).
All inputs are finite; a program needn't handle non-finite values.
Results may differ from a plain program's by a relative error of at most 0.011.
Values may be sent and summed in bfloat16 or wider, within the bound.
A program may use at most 64 MiB of HBM per device.

v0:
```python
import jax
import jax.numpy as jnp
from jax import lax
from jax.sharding import PartitionSpec as P

DH = 128


NEG_FILL = -1e30
BEYOND = 1 << 30


def extended(cells, sides, width):
    for axis, dim in sides:
        count = lax.axis_size(axis)
        ends = count - 1
        head = lax.slice_in_dim(cells, 0, width, axis=dim)
        tail = lax.slice_in_dim(cells, cells.shape[dim] - width, cells.shape[dim], axis=dim)
        cells = jnp.concatenate(
            [
                lax.ppermute(tail, axis, [(i, (i + 1) % count) for i in range(ends)]),
                cells,
                lax.ppermute(head, axis, [((i + 1) % count, i) for i in range(ends)]),
            ],
            axis=dim,
        )
    return cells


def split_heads(matrix, head_size):
    return matrix.reshape(matrix.shape[0], matrix.shape[1] // head_size, head_size)


def merge_heads(matrix):
    return matrix.reshape(matrix.shape[0], matrix.shape[1] * matrix.shape[2])


def contract(form, left, right):
    return jnp.einsum(form, left, right, preferred_element_type=jnp.float32)


def attend(queries, key_matrix, value_matrix, cotangent, present, score_scale):
    head_queries = split_heads(queries, DH)
    head_keys = split_heads(key_matrix, DH)
    head_values = split_heads(value_matrix, DH)
    head_cotangents = split_heads(cotangent, DH)
    scores = contract("qhd,khd->hqk", head_queries, head_keys) * score_scale
    scores = jnp.where(present[None], scores, NEG_FILL)
    highest = jnp.max(scores, axis=2, keepdims=True)
    exponent = jnp.where(present[None], jnp.exp(scores - highest), 0.0)
    probability = exponent / jnp.sum(exponent, axis=2, keepdims=True)
    weights = probability.astype(jnp.bfloat16)
    unrounded = contract("hqk,khd->qhd", weights, head_values)
    row_delta = jnp.sum(head_cotangents.astype(jnp.float32) * unrounded, axis=2)
    prob_grad = contract("qhd,khd->hqk", head_cotangents, head_values)
    score_grad = (probability * (prob_grad - jnp.transpose(row_delta)[:, :, None])).astype(
        jnp.bfloat16
    )
    query_grad = contract("hqk,khd->qhd", score_grad, head_keys) * score_scale
    key_grad = contract("hqk,qhd->khd", score_grad, head_queries) * score_scale
    value_grad = contract("hqk,qhd->khd", weights, head_cotangents)
    return (
        merge_heads(unrounded),
        merge_heads(query_grad),
        merge_heads(key_grad),
        merge_heads(value_grad),
    )


def local(
    video_query,
    video_key,
    video_value,
    video_cot,
    audio_query,
    audio_key,
    audio_value,
    audio_cot,
    intersection,
):
    video_rows, features = video_query.shape
    audio_rows = audio_query.shape[0]
    score_scale = DH ** (-0.5)
    position = lax.axis_index("video")
    padded_firsts = jnp.pad(intersection[:, 0], (1, 1), constant_values=BEYOND)
    padded_lasts = jnp.pad(intersection[:, 1], (1, 1), constant_values=-1)
    near_firsts = lax.dynamic_slice_in_dim(padded_firsts, position, 3, 0)
    near_lasts = lax.dynamic_slice_in_dim(padded_lasts, position, 3, 0)
    window_rows = (position - 1) * audio_rows + jnp.arange(3 * audio_rows, dtype=jnp.int32)
    audio_mask = (window_rows >= near_firsts[1]) & (window_rows < near_lasts[1])
    own_rows = position * audio_rows + jnp.arange(audio_rows, dtype=jnp.int32)
    row_blocks = (own_rows[None, :] >= near_firsts[:, None]) & (
        own_rows[None, :] < near_lasts[:, None]
    )
    span_rows = audio_rows + video_rows
    packed = jnp.concatenate(
        [
            jnp.concatenate([audio_key, audio_value], 1),
            jnp.concatenate([video_key, video_value], 1),
        ],
        0,
    )
    borders = extended(packed, (("video", 0),), span_rows)
    audio_window = jnp.concatenate(
        [
            borders[0:audio_rows],
            borders[span_rows : span_rows + audio_rows],
            borders[2 * span_rows : 2 * span_rows + audio_rows],
        ],
        0,
    )
    video_window = jnp.concatenate(
        [
            borders[audio_rows:span_rows],
            borders[span_rows + audio_rows : 2 * span_rows],
            borders[2 * span_rows + audio_rows : 3 * span_rows],
        ],
        0,
    )
    video_full, video_query_grad, audio_key_part, audio_value_part = attend(
        video_query,
        audio_window[:, :features],
        audio_window[:, features:],
        video_cot,
        audio_mask[None, :],
        score_scale,
    )
    audio_present = jnp.repeat(jnp.transpose(row_blocks), video_rows, axis=1)
    audio_full, audio_query_grad, video_key_part, video_value_part = attend(
        audio_query,
        video_window[:, :features],
        video_window[:, features:],
        audio_cot,
        audio_present,
        score_scale,
    )
    audio_pair = jnp.concatenate([audio_key_part, audio_value_part], 1)
    video_pair = jnp.concatenate([video_key_part, video_value_part], 1)
    outgoing = jnp.concatenate(
        [
            audio_pair[:audio_rows],
            video_pair[:video_rows],
            audio_pair[2 * audio_rows :],
            video_pair[2 * video_rows :],
        ],
        0,
    )
    returned = extended(outgoing, (("video", 0),), span_rows)
    arriving = returned[:span_rows] + returned[3 * span_rows :]
    audio_total = audio_pair[audio_rows : 2 * audio_rows] + arriving[:audio_rows]
    video_total = video_pair[video_rows : 2 * video_rows] + arriving[audio_rows:]
    audio_key_grad = audio_total[:, :features]
    audio_value_grad = audio_total[:, features:]
    video_key_grad = video_total[:, :features]
    video_value_grad = video_total[:, features:]
    return (
        video_full.astype(jnp.bfloat16),
        audio_full.astype(jnp.bfloat16),
        video_query_grad.astype(jnp.bfloat16),
        video_key_grad.astype(jnp.bfloat16),
        video_value_grad.astype(jnp.bfloat16),
        audio_query_grad.astype(jnp.bfloat16),
        audio_key_grad.astype(jnp.bfloat16),
        audio_value_grad.astype(jnp.bfloat16),
    )


def solution(mesh):
    return jax.shard_map(
        local,
        mesh=mesh,
        in_specs=(
            P(("clip", "video"), "audio"),
            P(("clip", "video"), "audio"),
            P(("clip", "video"), "audio"),
            P(("clip", "video"), "audio"),
            P(("clip", "video"), "audio"),
            P(("clip", "video"), "audio"),
            P(("clip", "video"), "audio"),
            P(("clip", "video"), "audio"),
            P("clip", None),
        ),
        out_specs=(
            P(("clip", "video"), "audio"),
            P(("clip", "video"), "audio"),
            P(("clip", "video"), "audio"),
            P(("clip", "video"), "audio"),
            P(("clip", "video"), "audio"),
            P(("clip", "video"), "audio"),
            P(("clip", "video"), "audio"),
            P(("clip", "video"), "audio"),
        ),
        check_vma=False,
    )
```

profile of v0, /device:TPU:1, one launch (start us, length us, event | category | flops | bytes accessed | tf_op | source)
XLA Modules:
  0.0 73.4 jit_solution(17210535165485237223)
XLA Ops:
  0.6 1.1 %copy.102 = bf16[128,768]{0,1:T(8,128)(2,1)S(1)} copy(bf16[128,768]{1,0:T(8,128)(2,1)} %param.10) | data formatting | bytes 393216 | tf_op args[1]
  1.8 1.1 %copy.103 = bf16[128,768]{0,1:T(8,128)(2,1)S(1)} copy(bf16[128,768]{1,0:T(8,128)(2,1)} %param.11) | data formatting | bytes 393216 | tf_op args[2]
  2.9 1.1 %copy.100 = bf16[64,768]{0,1:T(8,128)(2,1)S(1)} copy(bf16[64,768]{1,0:T(8,128)(2,1)} %param.14) | data formatting | bytes 196608 | tf_op args[5]
  3.9 1.1 %copy.101 = bf16[64,768]{0,1:T(8,128)(2,1)S(1)} copy(bf16[64,768]{1,0:T(8,128)(2,1)} %param.15) | data formatting | bytes 196608 | tf_op args[6]
  5.0 0.4 maximum_maximum_fusion
  5.4 1.1 %copy.104 = bf16[192,1536]{1,0:T(8,128)(2,1)} copy(bf16[192,1536]{0,1:T(8,128)(2,1)S(1)} %maximum_maximum_fusion) | data formatting | bytes 1179648 | tf_op jit(solution)/shard_map/concatenate | solution.py:96
  6.5 8.8 %collective-permute-start.1 = (bf16[192,1536]{1,0:T(8,128)(2,1)}, bf16[192,1536]{1,0:T(8,128)(2,1)S(1)}, u32[]{:S(2)}, u32[]{:S(2)}) collective-permute-start(bf16[192,1536]{1,0:T(8,128)(2,1)} %copy.104), channel_id=1, source_target_pairs={{4,0},{8,4},{12,8},{16,12},{20,16},{24,20},{28,24},{32,28},{36,32}... | collective-permute-start | bytes 1769480 | tf_op jit(solution)/shard_map/ppermute | solution.py:23
  15.3 1.9 %collective-permute-start = (bf16[192,1536]{1,0:T(8,128)(2,1)}, bf16[192,1536]{1,0:T(8,128)(2,1)S(1)}, u32[]{:S(2)}, u32[]{:S(2)}) collective-permute-start(bf16[192,1536]{1,0:T(8,128)(2,1)} %copy.104), channel_id=1, source_target_pairs={{0,4},{4,8},{8,12},{12,16},{16,20},{20,24},{24,28},{28,32},{32,36}... | collective-permute-start | bytes 1769480 | tf_op jit(solution)/shard_map/ppermute | solution.py:21
  17.3 0.6 slice.84
  17.9 0.6 slice.86
  18.8 0.6 copy.189
  19.6 0.8 %copy.121 = bf16[128,768]{0,1:T(8,128)(2,1)} copy(bf16[128,768]{1,0:T(8,128)(2,1)S(1)} %copy-done.12) | data formatting | bytes 393216 | tf_op args[3]
  20.4 1.3 %compare_and_fusion.1 = pred[192]{0:T(512)(128)(4,1)S(1)} fusion(s32[]{:T(128)} %bitcast.4, s32[]{:T(128)} %bitcast.2, s32[]{:T(128)S(6)} %mul.64), kind=kLoop, calls=%fused_computation.71 | loop fusion | flops 768 | bytes 204 | tf_op jit(solution)/shard_map/and | solution.py:90
  22.2 2.1 %collective-permute-done = bf16[192,1536]{1,0:T(8,128)(2,1)S(1)} collective-permute-done((bf16[192,1536]{1,0:T(8,128)(2,1)}, bf16[192,1536]{1,0:T(8,128)(2,1)S(1)}, u32[]{:S(2)}, u32[]{:S(2)}) %collective-permute-start) | collective-permute-done | bytes 589856 | tf_op jit(solution)/shard_map/ppermute | solution.py:21
  24.7 1.0 %fusion.44 = (bf16[384,768]{0,1:T(8,128)(2,1)S(1)}, bf16[384,768]{0,1:T(8,128)(2,1)}) fusion(bf16[384,1536]{0,1:T(8,128)(2,1)S(1)} %pad_maximum_fusion.1), kind=kLoop, calls=%fused_computation.78 | loop fusion | bytes 2359296 | tf_op jit(solution)/shard_map/slice | solution.py:131
  25.9 0.4 pad_maximum_fusion.3
  26.4 0.4 fusion.48
  26.8 0.5 copy-done.13
  27.3 1.1 %convolution_bitcast_fusion = f32[6,24,8,128]{3,2,1,0:T(8,128)} fusion(bf16[128,6,128]{0,2,1:T(8,128)(2,1)S(1)} %bitcast.141, f32[6,128,192]{1,2,0:T(8,128)S(1)} %get-tuple-element.57, f32[6,128]{1,0:T(8,128)S(1)} %get-tuple-element.56), kind=kOutput, calls=%fused_computation.20 | convolution fusion | flops 38043648 | bytes 1379328 | tf_op jit(solution)/shard_map/hqk,qhd->khd/dot_general | solution.py:39
  28.4 0.9 %multiply_reduce_fusion = (f32[128,6]{0,1:T(8,128)S(1)}, bf16[128,6,128]{0,2,1:T(8,128)(2,1)}) fusion(bf16[128,6,128]{0,2,1:T(8,128)(2,1)S(1)} %bitcast.142, bf16[192,6,128]{0,2,1:T(8,128)(2,1)S(1)} %bitcast.134, f32[6,128,192]{1,2,0:T(8,128)S(1)} %get-tuple-element.57, f32[6,128]{1,0:T(8,128)S(1)} %get-tuple-element.56), kind=kOutput, calls=%fused_computation.51 | convolution fusion | flops 38436096 | bytes 1284096 | tf_op jit(solution)/shard_map/hqk,khd->qhd/dot_general | solution.py:39
  29.3 0.3 fusion.18
  29.7 0.3 fusion.16
  30.0 0.6 copy-done.9
  30.9 1.0 %fusion.49 = (f32[6,64]{1,0:T(8,128)S(1)}, f32[6,64,384]{2,1,0:T(8,128)}) fusion(f32[6,64,384]{2,1,0:T(8,128)S(1)} %fusion.11, pred[64,384]{1,0:T(8,128)(4,1)S(1)} %bitcast.137), kind=kOutput, calls=%fused_computation.83 | output fusion | flops 442751 | bytes 1205760 | tf_op jit(solution)/shard_map/sub | solution.py:50
  31.9 1.9 %fusion.30 = f32[6,384,128]{1,2,0:T(8,128)} fusion(f32[6,64]{1,0:T(8,128)S(1)} %get-tuple-element.59, f32[6,64,384]{2,1,0:T(8,128)S(1)} %fusion.11, pred[64,384]{1,0:T(8,128)(4,1)S(1)} %bitcast.138, bf16[64,768]{1,0:T(8,128)(2,1)S(1)} %copy-done), kind=kOutput, calls=%fused_computation.59 | convolution fusion | flops 38339328 | bytes 1893888 | tf_op jit(solution)/shard_map/hqk,qhd->khd/dot_general | solution.py:39
  33.8 2.5 %multiply_reduce_fusion.1 = (f32[64,6]{0,1:T(8,128)S(1)}, bf16[6,8,8,128]{3,2,1,0:T(8,128)(2,1)}) fusion(bf16[384,6,128]{0,2,1:T(8,128)(2,1)} %bitcast.132, f32[6,64]{1,0:T(8,128)S(1)} %get-tuple-element.59, f32[6,64,384]{2,1,0:T(8,128)S(1)} %fusion.11, pred[64,384]{1,0:T(8,128)(4,1)S(1)} %bitcast.139, bf16[64,768]{1,0:T(8,128)(2,1)S(1)} %copy-done), kind=kOutput, calls=%fused_computation.56 | convolution fusion | flops 38535552 | bytes 1403904 | tf_op jit(solution)/shard_map/hqk,khd->qhd/dot_general | solution.py:39
  36.3 1.6 %copy.131 = f32[384,768]{1,0:T(8,128)S(1)} copy(f32[384,768]{0,1:T(8,128)} %bitcast.128) | data formatting | bytes 2359296 | tf_op jit(solution)/shard_map/reshape | solution.py:35
  38.0 1.2 %bitcast_dynamic-update-slice_fusion = f32[192,1536]{1,0:T(8,128)S(1)} fusion(f32[192,1536]{1,0:T(8,128)S(1)} %bitcast_dynamic-update-slice_fusion.1, f32[6,24,8,128]{3,2,1,0:T(8,128)} %convolution_bitcast_fusion), kind=kLoop, calls=%fused_computation.47 | loop fusion | bytes 1179648 | tf_op jit(solution)/shard_map/concatenate | solution.py:137
  39.2 1.0 %fusion.43 = (f32[64,1536]{1,0:T(8,128)}, f32[64,1536]{1,0:T(8,128)}) fusion(f32[192,1536]{1,0:T(8,128)S(1)} %bitcast_dynamic-update-slice_fusion), kind=kLoop, calls=%fused_computation.77 | loop fusion | bytes 1572864 | tf_op jit(solution)/shard_map/slice | solution.py:141
  40.5 1.4 %convolution_multiply_fusion = f32[6,384,128]{1,2,0:T(8,128)} fusion(bf16[6,64,384]{2,1,0:T(8,128)(2,1)S(1)} %fusion.17, bf16[64,768]{1,0:T(8,128)(2,1)S(1)} %copy-done.9), kind=kOutput, calls=%fused_computation.6 | convolution fusion | flops 38043648 | bytes 1572864 | tf_op jit(solution)/shard_map/hqk,qhd->khd/dot_general | solution.py:39
  41.9 1.6 %copy.130 = f32[384,768]{1,0:T(8,128)S(1)} copy(f32[384,768]{0,1:T(8,128)} %bitcast.125) | data formatting | bytes 2359296 | tf_op jit(solution)/shard_map/reshape | solution.py:35
  43.7 0.9 %copy-done.3 = f32[64,1536]{1,0:T(8,128)S(1)} copy-done((f32[64,1536]{1,0:T(8,128)S(1)}, f32[64,1536]{1,0:T(8,128)}, u32[]{:S(2)}) %copy-start.3) | copy-done | bytes 393240
  44.6 1.2 %fusion.19 = f32[192,1536]{1,0:T(8,128)} fusion(f32[384,768]{1,0:T(8,128)S(1)} %copy.131, f32[384,768]{1,0:T(8,128)S(1)} %copy.130, f32[64,1536]{1,0:T(8,128)S(1)} %copy-done.3), kind=kLoop, calls=%fused_computation.33 | loop fusion | flops 589824 | bytes 3932160 | tf_op jit(solution)/shard_map/concatenate | solution.py:139
  45.8 1.1 %pad_maximum_fusion.2 = f32[192,1536]{1,0:T(8,128)} fusion(f32[128,1536]{1,0:T(8,128)S(1)} %fusion.23, f32[64,1536]{1,0:T(8,128)S(1)} %copy-done.2), kind=kLoop, calls=%fused_computation.35 | loop fusion | flops 294912 | bytes 2359296 | tf_op jit(solution)/shard_map/concatenate | solution.py:139
  46.9 4.3 %collective-permute-start.2 = (f32[192,1536]{1,0:T(8,128)}, f32[192,1536]{1,0:T(8,128)}, u32[]{:S(2)}, u32[]{:S(2)}) collective-permute-start(f32[192,1536]{1,0:T(8,128)} %pad_maximum_fusion.2), channel_id=1, source_target_pairs={{0,4},{4,8},{8,12},{12,16},{16,20},{20,24},{24,28},{28,32},{32,36}... | collective-permute-start | bytes 3538952 | tf_op jit(solution)/shard_map/ppermute | solution.py:21
  51.2 1.9 %collective-permute-start.3 = (f32[192,1536]{1,0:T(8,128)}, f32[192,1536]{1,0:T(8,128)}, u32[]{:S(2)}, u32[]{:S(2)}) collective-permute-start(f32[192,1536]{1,0:T(8,128)} %fusion.19), channel_id=1, source_target_pairs={{4,0},{8,4},{12,8},{16,12},{20,16},{24,20},{28,24},{32,28},{36,32}... | collective-permute-start | bytes 3538952 | tf_op jit(solution)/shard_map/ppermute | solution.py:23
  53.1 0.9 %fusion.20 = bf16[6,128,128]{2,1,0:T(8,128)(2,1)} fusion(bf16[192,6,128]{0,2,1:T(8,128)(2,1)S(1)} %bitcast.127, bf16[6,128,192]{1,2,0:T(8,128)(2,1)S(1)} %copy-done.5), kind=kOutput, calls=%fused_computation.36 | convolution fusion | flops 37945344 | bytes 786432 | tf_op jit(solution)/shard_map/hqk,khd->qhd/dot_general | solution.py:39
  54.1 1.8 %copy.139 = bf16[128,768]{1,0:T(8,128)(2,1)} copy(bf16[128,768]{0,1:T(8,128)(2,1)} %bitcast.129) | data formatting | bytes 393216
  55.8 1.7 %copy.138 = bf16[128,768]{1,0:T(8,128)(2,1)} copy(bf16[128,768]{0,1:T(8,128)(2,1)} %bitcast.140) | data formatting | bytes 393216
  57.6 1.3 %fusion.22 = bf16[6,8,8,128]{3,2,1,0:T(8,128)(2,1)S(1)} fusion(bf16[384,6,128]{0,2,1:T(8,128)(2,1)S(1)} %bitcast.124, bf16[6,64,384]{2,1,0:T(8,128)(2,1)} %copy-done.6), kind=kOutput, calls=%fused_computation.40 | convolution fusion | flops 37847040 | bytes 983040 | tf_op jit(solution)/shard_map/hqk,khd->qhd/dot_general | solution.py:39
  58.9 0.7 copy.187
  59.6 0.7 copy.188
  60.3 4.4 %collective-permute-done.2 = f32[192,1536]{1,0:T(8,128)} collective-permute-done((f32[192,1536]{1,0:T(8,128)}, f32[192,1536]{1,0:T(8,128)}, u32[]{:S(2)}, u32[]{:S(2)}) %collective-permute-start.2) | collective-permute-done | bytes 1179680 | tf_op jit(solution)/shard_map/ppermute | solution.py:21
  64.6 4.4 %collective-permute-done.3 = f32[192,1536]{1,0:T(8,128)} collective-permute-done((f32[192,1536]{1,0:T(8,128)}, f32[192,1536]{1,0:T(8,128)}, u32[]{:S(2)}, u32[]{:S(2)}) %collective-permute-start.3) | collective-permute-done | bytes 1179680 | tf_op jit(solution)/shard_map/ppermute | solution.py:23
  69.0 1.8 %add.43 = f32[192,1536]{1,0:T(8,128)S(1)} add(f32[192,1536]{1,0:T(8,128)} %collective-permute-done.2, f32[192,1536]{1,0:T(8,128)} %collective-permute-done.3) | non-fusion elementwise | flops 294912 | bytes 3538944 | tf_op jit(solution)/shard_map/add | solution.py:149
  70.9 1.1 %fusion.27 = bf16[64,1536]{1,0:T(8,128)(2,1)S(1)} fusion(f32[192,1536]{1,0:T(8,128)S(1)} %add.43, f32[192,1536]{1,0:T(8,128)} %copy-done.1), kind=kLoop, calls=%fused_computation.50 | loop fusion | flops 196608 | bytes 983040 | tf_op jit(solution)/shard_map/convert.1
  72.0 0.7 fusion.47
  72.7 0.8 %fusion.46 = (bf16[128,768]{1,0:T(8,128)(2,1)}, bf16[128,768]{1,0:T(8,128)(2,1)}) fusion(bf16[128,1536]{1,0:T(8,128)(2,1)S(1)} %fusion.26), kind=kLoop, calls=%fused_computation.80 | loop fusion | bytes 786432 | tf_op jit(solution)/shard_map/slice | solution.py:155
  (52 shorter events, 2.6 us)
Async XLA Ops:
  0.6 31.3 %copy-start = (bf16[64,768]{1,0:T(8,128)(2,1)S(1)}, bf16[64,768]{1,0:T(8,128)(2,1)}, u32[]{:S(2)}) copy-start(bf16[64,768]{1,0:T(8,128)(2,1)} %param.16) | copy-start | bytes 294916
  5.0 12.2 %copy-start.15 = (s32[32,2]{0,1:T(2,128)S(1)}, s32[32,2]{0,1:T(2,128)}, u32[]{:S(2)}) copy-start(s32[32,2]{0,1:T(2,128)} %param.17) | copy-start | bytes 772
  5.0 14.4 %copy-start.11 = (bf16[128,768]{1,0:T(8,128)(2,1)S(1)}, bf16[128,768]{1,0:T(8,128)(2,1)}, u32[]{:S(2)}) copy-start(bf16[128,768]{1,0:T(8,128)(2,1)} %param.9) | copy-start | bytes 589828
  5.4 14.2 %copy-start.12 = (bf16[128,768]{1,0:T(8,128)(2,1)S(1)}, bf16[128,768]{1,0:T(8,128)(2,1)}, u32[]{:S(2)}) copy-start(bf16[128,768]{1,0:T(8,128)(2,1)} %param.12) | copy-start | bytes 589828
  6.5 15.2 %collective-permute-start.1 = (bf16[192,1536]{1,0:T(8,128)(2,1)}, bf16[192,1536]{1,0:T(8,128)(2,1)S(1)}, u32[]{:S(2)}, u32[]{:S(2)}) collective-permute-start(bf16[192,1536]{1,0:T(8,128)(2,1)} %copy.104), channel_id=1, source_target_pairs={{4,0},{8,4},{12,8},{16,12},{20,16},{24,20},{28,24},{32,28},{36,32}... | collective-permute-start | bytes 1769480 | tf_op jit(solution)/shard_map/ppermute | solution.py:23
  15.3 9.0 %collective-permute-start = (bf16[192,1536]{1,0:T(8,128)(2,1)}, bf16[192,1536]{1,0:T(8,128)(2,1)S(1)}, u32[]{:S(2)}, u32[]{:S(2)}) collective-permute-start(bf16[192,1536]{1,0:T(8,128)(2,1)} %copy.104), channel_id=1, source_target_pairs={{0,4},{4,8},{8,12},{12,16},{16,20},{20,24},{24,28},{28,32},{32,36}... | collective-permute-start | bytes 1769480 | tf_op jit(solution)/shard_map/ppermute | solution.py:21
  26.4 0.9 %copy-start.13 = (bf16[128,768]{0,1:T(8,128)(2,1)S(1)}, bf16[128,768]{0,1:T(8,128)(2,1)}, u32[]{:S(2)}) copy-start(bf16[128,768]{0,1:T(8,128)(2,1)} %copy.121) | copy-start | bytes 589828
  29.7 1.3 %copy-start.4 = (bf16[6,128,192]{1,2,0:T(8,128)(2,1)}, bf16[6,128,192]{1,2,0:T(8,128)(2,1)S(1)}, u32[]{:S(2)}) copy-start(bf16[6,128,192]{1,2,0:T(8,128)(2,1)S(1)} %fusion.18) | copy-start | bytes 884740
  29.7 1.0 %copy-start.9 = (bf16[64,768]{1,0:T(8,128)(2,1)S(1)}, bf16[64,768]{1,0:T(8,128)(2,1)}, u32[]{:S(2)}) copy-start(bf16[64,768]{1,0:T(8,128)(2,1)} %param.13) | copy-start | bytes 294916
  29.7 1.0 %copy-start.10 = (pred[8,8,3,128]{3,1,2,0:T(8,128)(4,1)S(1)}, pred[8,8,3,128]{3,1,2,0:T(8,128)(4,1)}, u32[]{:S(2)}) copy-start(pred[8,8,3,128]{3,1,2,0:T(8,128)(4,1)} %copy.189) | copy-start | bytes 73732
  38.0 2.3 %copy-start.7 = (f32[6,64,384]{2,1,0:T(8,128)S(1)}, f32[6,64,384]{2,1,0:T(8,128)}, u32[]{:S(2)}) copy-start(f32[6,64,384]{2,1,0:T(8,128)} %get-tuple-element.60) | copy-start | bytes 1769476
  38.0 2.3 %copy-start.8 = (bf16[384,768]{0,1:T(8,128)(2,1)S(1)}, bf16[384,768]{0,1:T(8,128)(2,1)}, u32[]{:S(2)}) copy-start(bf16[384,768]{0,1:T(8,128)(2,1)} %get-tuple-element.43) | copy-start | bytes 1769476
  39.2 1.3 %copy-start.1 = (f32[192,1536]{1,0:T(8,128)}, f32[192,1536]{1,0:T(8,128)S(1)}, u32[]{:S(2)}) copy-start(f32[192,1536]{1,0:T(8,128)S(1)} %bitcast_dynamic-update-slice_fusion) | copy-start | bytes 3538948
  40.5 1.4 %copy-start.6 = (bf16[6,64,384]{2,1,0:T(8,128)(2,1)}, bf16[6,64,384]{2,1,0:T(8,128)(2,1)S(1)}, u32[]{:S(2)}) copy-start(bf16[6,64,384]{2,1,0:T(8,128)(2,1)S(1)} %fusion.17) | copy-start | bytes 884740
  43.6 1.0 %copy-start.3 = (f32[64,1536]{1,0:T(8,128)S(1)}, f32[64,1536]{1,0:T(8,128)}, u32[]{:S(2)}) copy-start(f32[64,1536]{1,0:T(8,128)} %get-tuple-element.40) | copy-start | bytes 1179652
  44.6 1.2 %copy-start.2 = (f32[64,1536]{1,0:T(8,128)S(1)}, f32[64,1536]{1,0:T(8,128)}, u32[]{:S(2)}) copy-start(f32[64,1536]{1,0:T(8,128)} %get-tuple-element.41) | copy-start | bytes 1179652
  45.8 7.4 %copy-start.5 = (bf16[6,128,192]{1,2,0:T(8,128)(2,1)S(1)}, bf16[6,128,192]{1,2,0:T(8,128)(2,1)}, u32[]{:S(2)}) copy-start(bf16[6,128,192]{1,2,0:T(8,128)(2,1)} %copy-done.4) | copy-start | bytes 884740
  46.9 17.7 %collective-permute-start.2 = (f32[192,1536]{1,0:T(8,128)}, f32[192,1536]{1,0:T(8,128)}, u32[]{:S(2)}, u32[]{:S(2)}) collective-permute-start(f32[192,1536]{1,0:T(8,128)} %pad_maximum_fusion.2), channel_id=1, source_target_pairs={{0,4},{4,8},{8,12},{12,16},{16,20},{20,24},{24,28},{28,32},{32,36}... | collective-permute-start | bytes 3538952 | tf_op jit(solution)/shard_map/ppermute | solution.py:21
  51.2 17.8 %collective-permute-start.3 = (f32[192,1536]{1,0:T(8,128)}, f32[192,1536]{1,0:T(8,128)}, u32[]{:S(2)}, u32[]{:S(2)}) collective-permute-start(f32[192,1536]{1,0:T(8,128)} %fusion.19), channel_id=1, source_target_pairs={{4,0},{8,4},{12,8},{16,12},{20,16},{24,20},{28,24},{32,28},{36,32}... | collective-permute-start | bytes 3538952 | tf_op jit(solution)/shard_map/ppermute | solution.py:23
  54.1 5.5 %copy-start.14 = (bf16[6,8,8,128]{3,2,1,0:T(8,128)(2,1)S(1)}, bf16[6,8,8,128]{3,2,1,0:T(8,128)(2,1)}, u32[]{:S(2)}) copy-start(bf16[6,8,8,128]{3,2,1,0:T(8,128)(2,1)} %get-tuple-element.53) | copy-start | bytes 294916
where the time goes:
time: 74.1 us; the launch traced here: 73.4 us
  local copies, waits for them, and re-layouts  24.5 us (33%)
  starting transfers between devices  16.9 us (23%)
  matrix products  11.6 us (16%)
  waiting for transfers between devices  10.8 us (15%)
  other arithmetic  8.63 us (12%)
  between operations  1.01 us (1%)
    unnamed x46, local copies, waits for them, and re-layouts  12.5 us
    dot_general x11, matrix products, contract(): return jnp.einsum(form, left, right, preferred_element_type=jnp.float32)  11.2 us
    ppermute x2, starting transfers between devices, extended(): lax.ppermute(head, axis, [((i + 1) % count, i) for i in range(ends)])  10.7 us
    ppermute x2, waiting for transfers between devices, extended(): lax.ppermute(tail, axis, [(i, (i + 1) % count) for i in range(ends)])  6.44 us
    ppermute x2, starting transfers between devices, extended(): lax.ppermute(tail, axis, [(i, (i + 1) % count) for i in range(ends)])  6.19 us
    ppermute x2, waiting for transfers between devices, extended(): lax.ppermute(head, axis, [((i + 1) % count, i) for i in range(ends)])  4.4 us
    reshape x2, local copies, waits for them, and re-layouts, merge_heads(): return matrix.reshape(matrix.shape[0], matrix.shape[1] * matrix.shape[2])  3.27 us
    concatenate x2, other arithmetic, local(): jnp.concatenate([audio_pair[:audio_rows], video_pair[:video_rows], audio_...  2.32 us
  transfers between devices with their start and end apart: 4, of which 3 were waited for; matrix products, arithmetic and copies ran while one was open for 16% of the time, Pallas kernels for 0%

commit v1 on v0

v1 whole, which is shorter than its diff:
```python
import functools

import jax
import jax.numpy as jnp
from jax import lax
from jax.experimental import pallas as pl
from jax.experimental.pallas import tpu as pltpu
from jax.sharding import PartitionSpec as P

DH = 128
NEG = -1e30
LOG2E = 1.4426950408889634
MESH = pl.DeviceIdType.MESH
F32 = jnp.float32
BF16 = jnp.bfloat16
Q, K, V, C = 0, 1, 2, 3
DK, DV, OUT, DQ = 0, 1, 2, 3
CHUNKS = 3


def dot_nt(a, b):
    return lax.dot_general(a, b, (((1,), (1,)), ((), ())), preferred_element_type=F32)


def dot_nn(a, b):
    return lax.dot_general(a, b, (((1,), (0,)), ((), ())), preferred_element_type=F32)


def dot_tn(a, b):
    return lax.dot_general(a, b, (((0,), (0,)), ((), ())), preferred_element_type=F32)


def joined(parts):
    top = functools.reduce(jnp.maximum, [p[0] for p in parts])
    total = sum(p[1] * jnp.exp2(p[0] - top) for p in parts)
    weighted = sum(p[2] * jnp.exp2(p[0] - top) for p in parts)
    inverse = jnp.where(total > 0, 1.0 / jnp.where(total > 0, total, 1.0), 0.0)
    return jnp.exp2(parts[0][0] - top) * inverse, weighted * inverse


def kernel(blocks, vrows, arows, heads, *refs):
    (vq, vk, vv, vc, aq, ak, av, ac, inter, out) = refs[:10]
    (vid, win, e_on, dp_on, e_far, dp_far, p1, ds1, p2, ds2, own, s_near, s_far, r_near, r_far,
     es, ls, re_n, re_f, re_fn, rl_f, rl_nf, fac_on, fac_far, bias,
     load_sem, near_sem, far_ssem, far_rsem, es_ssem, es_rsem, ls_ssem, ls_rsem,
     kv_ssem, kv_rsem, oq_ssem, oq_rsem, nr_ssem, nr_rsem) = refs[10:]
    scale = DH ** (-0.5)
    scale2 = scale * LOG2E
    two = 2 * arows
    three = 3 * arows

    b = lax.axis_index("video")
    odd = lax.rem(b, 2)
    n = b + 1 - 2 * odd
    f = b - 1 + 2 * odd
    nf = n - 1 + 2 * (1 - odd)
    fn = f + 1 - 2 * (1 - odd)
    has_f = (f >= 0) & (f < blocks)
    has_nf = (nf >= 0) & (nf < blocks)

    def here(index):
        return {"video": index}

    barrier = pltpu.get_barrier_semaphore()
    pl.semaphore_signal(barrier, inc=1, device_id=here(n), device_id_type=MESH)

    @pl.when(has_f)
    def _():
        pl.semaphore_signal(barrier, inc=1, device_id=here(f), device_id_type=MESH)
        pl.semaphore_signal(barrier, inc=1, device_id=here(fn), device_id_type=MESH)

    @pl.when(has_nf)
    def _():
        pl.semaphore_signal(barrier, inc=1, device_id=here(nf), device_id_type=MESH)

    loads = []
    for t, ref in enumerate((aq, ak, av, ac)):
        loads.append(pltpu.make_async_copy(ref, win.at[t, pl.ds(0, arows)], load_sem.at[t]))
    for t, ref in enumerate((vq, vk, vv, vc)):
        loads.append(pltpu.make_async_copy(ref, vid.at[t], load_sem.at[4 + t]))
    for copy in loads:
        copy.start()

    first, last = inter[b, 0], inter[b, 1]
    lane = lax.broadcasted_iota(jnp.int32, (1, DH), 1)
    rows_on = jnp.where(lane < arows, b * arows + lane, n * arows + lane - arows)
    mask_on = (rows_on >= first) & (rows_on < last)
    lane_far = lax.broadcasted_iota(jnp.int32, (1, arows), 1)
    rows_far = f * arows + lane_far
    mask_far = (rows_far >= first) & (rows_far < last)
    sub = lax.broadcasted_iota(jnp.int32, (three, DH), 0)
    rows_sub = jnp.where(sub < arows, b * arows + sub,
                         jnp.where(sub < two, n * arows + sub - arows, f * arows + sub - two))
    bias[...] = jnp.where((rows_sub >= first) & (rows_sub < last), 0.0, NEG)

    es[...] = jnp.zeros_like(es)
    ls[...] = jnp.zeros_like(ls)

    @pl.when(jnp.logical_not(has_f))
    def _():
        for t in range(4):
            win[t, pl.ds(two, arows), :] = jnp.zeros((arows, heads * DH), BF16)
            r_far[t] = jnp.zeros((arows, heads * DH), BF16)
        for ref in (re_f, re_fn, rl_f):
            ref[0] = jnp.full(ref.shape[1:], NEG, F32)
            ref[1] = jnp.zeros(ref.shape[1:], F32)
            ref[2] = jnp.zeros(ref.shape[1:], F32)

    @pl.when(jnp.logical_not(has_nf))
    def _():
        rl_nf[0] = jnp.full(rl_nf.shape[1:], NEG, F32)
        rl_nf[1] = jnp.zeros(rl_nf.shape[1:], F32)
        rl_nf[2] = jnp.zeros(rl_nf.shape[1:], F32)

    def remote(src, dst, ssem, rsem, device):
        return pltpu.make_async_remote_copy(
            src_ref=src, dst_ref=dst, send_sem=ssem, recv_sem=rsem, device_id=here(device), device_id_type=MESH
        )

    per = heads // CHUNKS
    width = per * DH

    def chunk_cols(c):
        return pl.ds(c * width, width)

    near_in = remote(win.at[:, pl.ds(0, arows)], win.at[:, pl.ds(arows, arows)], near_sem.at[0], near_sem.at[1], n)
    far_in = [
        remote(win.at[:, pl.ds(0, arows), chunk_cols(c)], win.at[:, pl.ds(two, arows), chunk_cols(c)],
               far_ssem.at[c], far_rsem.at[c], f)
        for c in range(CHUNKS)
    ]
    es_n = remote(es, re_n, es_ssem.at[0], es_rsem.at[0], n)
    es_f = remote(es, re_f, es_ssem.at[1], es_rsem.at[1], f)
    es_nf = remote(es, re_fn, es_ssem.at[2], es_rsem.at[2], nf)
    ls_f = remote(ls, rl_f, ls_ssem.at[0], ls_rsem.at[0], f)
    ls_fn = remote(ls, rl_nf, ls_ssem.at[1], ls_rsem.at[1], fn)
    kv_far = [
        remote(s_far.at[pl.ds(0, 2), :, chunk_cols(c)], r_far.at[pl.ds(0, 2), :, chunk_cols(c)],
               kv_ssem.at[c], kv_rsem.at[c], f)
        for c in range(CHUNKS)
    ]
    oq_far = [
        remote(s_far.at[pl.ds(2, 2), :, chunk_cols(c)], r_far.at[pl.ds(2, 2), :, chunk_cols(c)],
               oq_ssem.at[c], oq_rsem.at[c], f)
        for c in range(CHUNKS)
    ]
    kv_near = remote(s_near.at[pl.ds(0, 2)], r_near.at[pl.ds(0, 2)], nr_ssem.at[0], nr_rsem.at[0], n)
    oq_near = remote(s_near.at[pl.ds(2, 2)], r_near.at[pl.ds(2, 2)], nr_ssem.at[1], nr_rsem.at[1], n)

    for copy in loads[:4]:
        copy.wait()
    pl.semaphore_wait(barrier, 1 + 2 * has_f.astype(jnp.int32) + has_nf.astype(jnp.int32))

    @pl.when(has_f)
    def _():
        for c in range(CHUNKS - 1):
            far_in[c].start()

    near_in.start()
    for copy in loads[4:]:
        copy.wait()
    near_in.wait_recv()

    for h in range(heads):
        cols = pl.ds(h * DH, DH)
        s = dot_nt(vid[K, :, cols], win[Q, pl.ds(0, two), cols]) * scale2
        dp = dot_nt(vid[V, :, cols], win[C, pl.ds(0, two), cols])
        top = jnp.max(s, axis=0, keepdims=True)
        e = jnp.exp2(s - top)
        e_on[h] = e
        dp_on[h] = dp
        es[0, pl.ds(h, 1), :] = jnp.where(mask_on, top, NEG)
        es[1, pl.ds(h, 1), :] = jnp.where(mask_on, jnp.sum(e, axis=0, keepdims=True), 0.0)
        es[2, pl.ds(h, 1), :] = jnp.where(mask_on, jnp.sum(e * dp, axis=0, keepdims=True), 0.0)

    @pl.when(has_f)
    def _():
        es_f.start()

    @pl.when(has_nf)
    def _():
        es_nf.start()

    es_n.start()

    @pl.when(has_f)
    def _():
        far_in[CHUNKS - 1].start()

    def stage_scores(c):
        @pl.when(has_f)
        def _():
            far_in[c].wait_recv()

        for h in range(c * per, (c + 1) * per):
            cols = pl.ds(h * DH, DH)
            qv, cv = vid[Q, :, cols], vid[C, :, cols]
            s = dot_nt(win[K, :, cols], qv) * scale2 + bias[...]
            dp = dot_nt(win[V, :, cols], cv)
            top = jnp.max(s, axis=0, keepdims=True)
            e = jnp.exp2(s - top)
            inverse = 1.0 / jnp.sum(e, axis=0, keepdims=True)
            prob = e * inverse
            delta = jnp.sum(prob * dp, axis=0, keepdims=True)
            weights = prob.astype(BF16)
            dscore = (prob * (dp - delta)).astype(BF16)
            p1[h] = weights
            ds1[h] = dscore
            s_far[DK, :, cols] = (dot_nn(dscore[two:], qv) * scale).astype(BF16)
            s_far[DV, :, cols] = dot_nn(weights[two:], cv).astype(BF16)

        @pl.when(has_f)
        def _():
            kv_far[c].start()

        for h in range(c * per, (c + 1) * per):
            cols = pl.ds(h * DH, DH)
            s = dot_nt(vid[K, :, cols], win[Q, pl.ds(two, arows), cols]) * scale2
            dp = dot_nt(vid[V, :, cols], win[C, pl.ds(two, arows), cols])
            top = jnp.max(s, axis=0, keepdims=True)
            e = jnp.exp2(s - top)
            e_far[h] = e
            dp_far[h] = dp
            ls[0, pl.ds(h, 1), pl.ds(0, arows)] = jnp.where(mask_far, top, NEG)
            ls[1, pl.ds(h, 1), pl.ds(0, arows)] = jnp.where(mask_far, jnp.sum(e, axis=0, keepdims=True), 0.0)
            ls[2, pl.ds(h, 1), pl.ds(0, arows)] = jnp.where(mask_far, jnp.sum(e * dp, axis=0, keepdims=True), 0.0)

    def wait_early():
        @pl.when(has_f)
        def _():
            es_f.wait_recv()
            es_nf.wait_recv()

    def stage_far(c):
        factor, delta = joined([
            [ls[i] for i in range(3)],
            [re_f[i] for i in range(3)],
            [pltpu.roll(re_fn[i], arows, 1) for i in range(3)],
        ])
        fac_far[0] = factor
        fac_far[1] = delta
        for h in range(c * per, (c + 1) * per):
            cols = pl.ds(h * DH, DH)
            prob = e_far[h] * fac_far[0, pl.ds(h, 1), pl.ds(0, arows)]
            weights = prob.astype(BF16)
            dscore = (prob * (dp_far[h] - fac_far[1, pl.ds(h, 1), pl.ds(0, arows)])).astype(BF16)
            p2[h, :, pl.ds(two, arows)] = weights
            ds2[h, :, pl.ds(two, arows)] = dscore
            s_far[OUT, :, cols] = dot_tn(weights, vid[V, :, cols]).astype(BF16)
            s_far[DQ, :, cols] = (dot_tn(dscore, vid[K, :, cols]) * scale).astype(BF16)

        @pl.when(has_f)
        def _():
            oq_far[c].start()

    stage_scores(0)
    stage_scores(1)
    wait_early()
    stage_far(0)
    stage_far(1)
    stage_scores(2)

    @pl.when(has_f)
    def _():
        ls_f.start()
        ls_fn.start()

    stage_far(2)

    for h in range(heads):
        cols = pl.ds(h * DH, DH)
        dk = dot_nn(ds1[h, pl.ds(0, two), :], vid[Q, :, cols]) * scale
        dv = dot_nn(p1[h, pl.ds(0, two), :], vid[C, :, cols])
        own[DK, :, cols] = dk[:arows]
        own[DV, :, cols] = dv[:arows]
        s_near[DK, :, cols] = dk[arows:].astype(BF16)
        s_near[DV, :, cols] = dv[arows:].astype(BF16)
    kv_near.start()

    def place(index):
        starts = [0, vrows, vrows + arows, 2 * vrows + arows, 3 * vrows + arows,
                  4 * vrows + arows, 4 * vrows + 2 * arows, 4 * vrows + 3 * arows]
        return pl.ds(starts[index], arows if index in (1, 5, 6, 7) else vrows)

    for h in range(heads):
        cols = pl.ds(h * DH, DH)
        out[place(0), cols] = dot_tn(p1[h], win[V, :, cols]).astype(BF16)
        out[place(2), cols] = (dot_tn(ds1[h], win[K, :, cols]) * scale).astype(BF16)

    es_n.wait_recv()

    @pl.when(has_f)
    def _():
        ls_f.wait_recv()

    @pl.when(has_nf)
    def _():
        ls_fn.wait_recv()

    left = lax.broadcasted_iota(jnp.int32, (8, DH), 1) < arows
    factor, delta = joined([
        [es[i] for i in range(3)],
        [pltpu.roll(re_n[i], arows, 1) for i in range(3)],
        [jnp.where(left, rl_f[i], pltpu.roll(rl_nf[i], arows, 1)) for i in range(3)],
    ])
    fac_on[0] = factor
    fac_on[1] = delta
    for h in range(heads):
        cols = pl.ds(h * DH, DH)
        prob = e_on[h] * fac_on[0, pl.ds(h, 1), :]
        weights = prob.astype(BF16)
        dscore = (prob * (dp_on[h] - fac_on[1, pl.ds(h, 1), :])).astype(BF16)
        p2[h, :, pl.ds(0, two)] = weights
        ds2[h, :, pl.ds(0, two)] = dscore
        o = dot_tn(weights, vid[V, :, cols])
        dq = dot_tn(dscore, vid[K, :, cols]) * scale
        own[OUT, :, cols] = o[:arows]
        own[DQ, :, cols] = dq[:arows]
        s_near[OUT, :, cols] = o[arows:].astype(BF16)
        s_near[DQ, :, cols] = dq[arows:].astype(BF16)
    oq_near.start()

    for h in range(heads):
        cols = pl.ds(h * DH, DH)
        out[place(3), cols] = (dot_nn(ds2[h, :, pl.ds(0, three)], win[Q, :, cols]) * scale).astype(BF16)
        out[place(4), cols] = dot_nn(p2[h, :, pl.ds(0, three)], win[C, :, cols]).astype(BF16)

    kv_near.wait_recv()
    oq_near.wait_recv()
    for c in range(CHUNKS):
        for pair, copies in (((DK, DV), kv_far), ((OUT, DQ), oq_far)):
            @pl.when(has_f)
            def _(copy=copies[c]):
                copy.wait_recv()

            for t in pair:
                cols = chunk_cols(c)
                total = own[t, :, cols] + r_near[t, :, cols].astype(F32) + r_far[t, :, cols].astype(F32)
                out[place({OUT: 1, DQ: 5, DK: 6, DV: 7}[t]), cols] = total.astype(BF16)

    near_in.wait_send()
    es_n.wait_send()
    kv_near.wait_send()
    oq_near.wait_send()

    @pl.when(has_f)
    def _():
        for copy in (*far_in, *kv_far, *oq_far, es_f, ls_f, ls_fn):
            copy.wait_send()

    @pl.when(has_nf)
    def _():
        es_nf.wait_send()


def spread(sizes, joint, *refs):
    outs, sems = refs[: len(sizes)], refs[len(sizes)]
    start, copies = 0, []
    for index, size in enumerate(sizes):
        copies.append(pltpu.make_async_copy(joint.at[pl.ds(start, size)], outs[index], sems.at[index]))
        start += size
    for copy in copies:
        copy.start()
    for copy in copies:
        copy.wait()


def local(video_query, video_key, video_value, video_cot, audio_query, audio_key, audio_value, audio_cot, intersection):
    vrows, features = video_query.shape
    arows = audio_query.shape[0]
    heads = features // DH
    blocks = lax.axis_size("video")
    sizes = [vrows, arows, vrows, vrows, vrows, arows, arows, arows]
    dma = pltpu.SemaphoreType.DMA
    audio = (4, arows, features)
    scratch = [
        pltpu.VMEM((4, vrows, features), BF16),
        pltpu.VMEM((4, 3 * arows, features), BF16),
        pltpu.VMEM((heads, vrows, 2 * arows), F32),
        pltpu.VMEM((heads, vrows, 2 * arows), F32),
        pltpu.VMEM((heads, vrows, arows), F32),
        pltpu.VMEM((heads, vrows, arows), F32),
        pltpu.VMEM((heads, 3 * arows, vrows), BF16),
        pltpu.VMEM((heads, 3 * arows, vrows), BF16),
        pltpu.VMEM((heads, vrows, 4 * arows), BF16),
        pltpu.VMEM((heads, vrows, 4 * arows), BF16),
        pltpu.VMEM(audio, F32),
        pltpu.VMEM(audio, BF16),
        pltpu.VMEM(audio, BF16),
        pltpu.VMEM(audio, BF16),
        pltpu.VMEM(audio, BF16),
        *[pltpu.VMEM((3, 8, DH), F32)] * 7,
        *[pltpu.VMEM((2, 8, DH), F32)] * 2,
        pltpu.VMEM((3 * arows, DH), F32),
        dma((8,)),
        dma((2,)),
        dma((CHUNKS,)),
        dma((CHUNKS,)),
        dma((3,)),
        dma((3,)),
        dma((2,)),
        dma((2,)),
        dma((CHUNKS,)),
        dma((CHUNKS,)),
        dma((CHUNKS,)),
        dma((CHUNKS,)),
        dma((2,)),
        dma((2,)),
    ]
    any_space = pl.BlockSpec(memory_space=pl.ANY)
    joint = pl.pallas_call(
        functools.partial(kernel, blocks, vrows, arows, heads),
        out_shape=pltpu.VMEM((sum(sizes), features), BF16),
        in_specs=[any_space] * 8 + [pl.BlockSpec(memory_space=pltpu.SMEM)],
        out_specs=pl.BlockSpec(memory_space=pltpu.VMEM),
        scratch_shapes=scratch,
        compiler_params=pltpu.CompilerParams(
            collective_id=0, has_side_effects=True, vmem_limit_bytes=24 * 1024 * 1024
        ),
        cost_estimate=pl.CostEstimate(
            flops=24 * heads * vrows * 3 * arows * DH, bytes_accessed=12 * (vrows + arows) * features, transcendentals=0
        ),
        name="cross_attention",
    )(video_query, video_key, video_value, video_cot, audio_query, audio_key, audio_value, audio_cot, intersection)
    joint = pltpu.with_memory_space_constraint(joint, pltpu.VMEM)
    return tuple(
        pl.pallas_call(
            functools.partial(spread, sizes),
            out_shape=[jax.ShapeDtypeStruct((size, features), BF16) for size in sizes],
            in_specs=[any_space],
            out_specs=[any_space] * len(sizes),
            scratch_shapes=[dma((len(sizes),))],
            name="spread",
        )(joint)
    )


def solution(mesh):
    rows = P(("clip", "video"), "audio")
    return jax.shard_map(
        local,
        mesh=mesh,
        in_specs=(rows,) * 8 + (P("clip", None),),
        out_specs=(rows,) * 8,
        check_vma=False,
    )
```

time: 74.1 us -> 32.2 us (0.43)
  Pallas kernels: 0 us -> 23.2 us
  starting transfers between devices: 16.9 us -> 0 us
  local copies, waits for them, and re-layouts: 24.5 us -> 8.03 us
  matrix products: 11.6 us -> 0 us
  waiting for transfers between devices: 10.8 us -> 0 us
  other arithmetic: 8.63 us -> 0 us
    pallas_call x0 -> x2, Pallas kernels: none -> 23.2 us  [the longest x1 22.1 us: local(): pl.pallas_call(functools.partial(kernel, blocks, vrows, arows, heads), ou...]
    ppermute x4 -> x0, starting transfers between devices: 16.9 us -> none  [the longest x2 10.7 us: extended(): lax.ppermute(head, axis, [((i + 1) % count, i) for i in range(ends)])]
    dot_general x11 -> x0, matrix products: 11.2 us -> none  [contract(): return jnp.einsum(form, left, right, preferred_element_type=jnp.float32)]
    ppermute x4 -> x0, waiting for transfers between devices: 10.8 us -> none  [the longest x2 6.44 us: extended(): lax.ppermute(tail, axis, [(i, (i + 1) % count) for i in range(ends)])]
    slice x11 -> x0, local copies, waits for them, and re-layouts: 4.73 us -> none  [the longest x2 1.17 us: local(): audio_mask = (window_rows >= near_firsts[1]) & (window_rows < near_lasts[1])]
    unnamed x46 -> x17, local copies, waits for them, and re-layouts: 12.5 us -> 8.03 us
    concatenate x6 -> x0, other arithmetic: 3.31 us -> none  [the longest x2 2.32 us: local(): jnp.concatenate([audio_pair[:audio_rows], video_pair[:video_rows], audio_...]
    reshape x2 -> x0, local copies, waits for them, and re-layouts: 3.27 us -> none  [merge_heads(): return matrix.reshape(matrix.shape[0], matrix.shape[1] * matrix.shape[2])]
  transfers between devices with their start and end apart: 4 -> 0, of which waited for: 3 -> 0; matrix products, arithmetic and copies ran while one was open for 16% -> 0% of each run, Pallas kernels for 0% -> 0%
where the time goes in v1:
time: 32.2 us; the launch traced here: 31.9 us
  Pallas kernels  23.2 us (72%)
  local copies, waits for them, and re-layouts  8.03 us (25%)
  between operations  0.65 us (2%)
    pallas_call x1, Pallas kernels, local(): pl.pallas_call(functools.partial(kernel, blocks, vrows, arows, heads), ou...  22.1 us
    unnamed x17, local copies, waits for them, and re-layouts  8.03 us
    pallas_call x1, Pallas kernels, local(): pl.pallas_call(functools.partial(spread, sizes), out_shape=[jax.ShapeDtyp...  1.07 us

profile of v1, /device:TPU:1, one launch (start us, length us, event | category | flops | bytes accessed | tf_op | source)
XLA Modules:
  0.0 31.9 jit_solution(7877495956590898890)
XLA Ops:
  0.6 0.8 %copy.17.refs_8_ = s32[32,2]{1,0:T(8,128)S(1)} copy(s32[32,2]{0,1:T(2,128)} %param.17) | data formatting | bytes 512 | tf_op args[8]
  1.4 0.0 copy-start
  1.4 0.9 %copy-done = bf16[128,768]{1,0:T(8,128)(2,1)S(1)} copy-done((bf16[128,768]{1,0:T(8,128)(2,1)S(1)}, bf16[128,768]{1,0:T(8,128)(2,1)}, u32[]{:S(2)}) %copy-start) | copy-done | bytes 196632
  2.3 0.0 copy-start.1
  2.3 0.9 %copy-done.1 = bf16[128,768]{1,0:T(8,128)(2,1)S(1)} copy-done((bf16[128,768]{1,0:T(8,128)(2,1)S(1)}, bf16[128,768]{1,0:T(8,128)(2,1)}, u32[]{:S(2)}) %copy-start.1) | copy-done | bytes 196632
  3.2 0.0 copy-start.2
  3.2 0.9 %copy-done.2 = bf16[128,768]{1,0:T(8,128)(2,1)S(1)} copy-done((bf16[128,768]{1,0:T(8,128)(2,1)S(1)}, bf16[128,768]{1,0:T(8,128)(2,1)}, u32[]{:S(2)}) %copy-start.2) | copy-done | bytes 196632
  4.2 0.0 copy-start.3
  4.2 0.9 %copy-done.3 = bf16[128,768]{1,0:T(8,128)(2,1)S(1)} copy-done((bf16[128,768]{1,0:T(8,128)(2,1)S(1)}, bf16[128,768]{1,0:T(8,128)(2,1)}, u32[]{:S(2)}) %copy-start.3) | copy-done | bytes 196632
  5.1 0.0 copy-start.4
  5.1 0.9 %copy-done.4 = bf16[64,768]{1,0:T(8,128)(2,1)S(1)} copy-done((bf16[64,768]{1,0:T(8,128)(2,1)S(1)}, bf16[64,768]{1,0:T(8,128)(2,1)}, u32[]{:S(2)}) %copy-start.4) | copy-done | bytes 98328
  6.0 0.0 copy-start.5
  6.0 0.9 %copy-done.5 = bf16[64,768]{1,0:T(8,128)(2,1)S(1)} copy-done((bf16[64,768]{1,0:T(8,128)(2,1)S(1)}, bf16[64,768]{1,0:T(8,128)(2,1)}, u32[]{:S(2)}) %copy-start.5) | copy-done | bytes 98328
  6.9 0.0 copy-start.6
  6.9 0.9 %copy-done.6 = bf16[64,768]{1,0:T(8,128)(2,1)S(1)} copy-done((bf16[64,768]{1,0:T(8,128)(2,1)S(1)}, bf16[64,768]{1,0:T(8,128)(2,1)}, u32[]{:S(2)}) %copy-start.6) | copy-done | bytes 98328
  7.8 0.0 copy-start.7
  7.8 0.9 %copy-done.7 = bf16[64,768]{1,0:T(8,128)(2,1)S(1)} copy-done((bf16[64,768]{1,0:T(8,128)(2,1)S(1)}, bf16[64,768]{1,0:T(8,128)(2,1)}, u32[]{:S(2)}) %copy-start.7) | copy-done | bytes 98328
  8.7 22.1 %cross_attention.1.joint = bf16[768,768]{1,0:T(8,128)(2,1)S(1)} custom-call(bf16[128,768]{1,0:T(8,128)(2,1)S(1)} %copy-done, bf16[128,768]{1,0:T(8,128)(2,1)S(1)} %copy-done.1, bf16[128,768]{1,0:T(8,128)(2,1)S(1)} %copy-done.2, bf16[128,768]{1,0:T(8,128)(2,1)S(1)} %copy-done.3, bf16[64,768]{1,0:T(8,128)(2,1)S(1)} %copy-done.4, ...), custom_call_target="tpu_custom_call" | custom-call | flops 452984832 | bytes 1769472 | tf_op jit(solution)/shard_map/cross_attention/pallas_call | solution.py:411
  30.8 1.1 %spread.1 = (bf16[128,768]{1,0:T(8,128)(2,1)}, bf16[64,768]{1,0:T(8,128)(2,1)}, bf16[128,768]{1,0:T(8,128)(2,1)}, bf16[128,768]{1,0:T(8,128)(2,1)}, bf16[128,768...) custom-call(bf16[768,768]{1,0:T(8,128)(2,1)S(1)} %cross_attention.1.joint), custom_call_target="tpu_custom_call" | custom-call | tf_op jit(solution)/shard_map/spread/pallas_call | solution.py:427
Async XLA Ops:
  1.4 0.9 %copy-start = (bf16[128,768]{1,0:T(8,128)(2,1)S(1)}, bf16[128,768]{1,0:T(8,128)(2,1)}, u32[]{:S(2)}) copy-start(bf16[128,768]{1,0:T(8,128)(2,1)} %refs_0_.1) | copy-start | bytes 589828
  2.3 0.9 %copy-start.1 = (bf16[128,768]{1,0:T(8,128)(2,1)S(1)}, bf16[128,768]{1,0:T(8,128)(2,1)}, u32[]{:S(2)}) copy-start(bf16[128,768]{1,0:T(8,128)(2,1)} %refs_1_.1) | copy-start | bytes 589828
  3.2 0.9 %copy-start.2 = (bf16[128,768]{1,0:T(8,128)(2,1)S(1)}, bf16[128,768]{1,0:T(8,128)(2,1)}, u32[]{:S(2)}) copy-start(bf16[128,768]{1,0:T(8,128)(2,1)} %refs_2_.1) | copy-start | bytes 589828
  4.2 0.9 %copy-start.3 = (bf16[128,768]{1,0:T(8,128)(2,1)S(1)}, bf16[128,768]{1,0:T(8,128)(2,1)}, u32[]{:S(2)}) copy-start(bf16[128,768]{1,0:T(8,128)(2,1)} %refs_3_.1) | copy-start | bytes 589828
  5.1 0.9 %copy-start.4 = (bf16[64,768]{1,0:T(8,128)(2,1)S(1)}, bf16[64,768]{1,0:T(8,128)(2,1)}, u32[]{:S(2)}) copy-start(bf16[64,768]{1,0:T(8,128)(2,1)} %refs_4_.1) | copy-start | bytes 294916
  6.0 0.9 %copy-start.5 = (bf16[64,768]{1,0:T(8,128)(2,1)S(1)}, bf16[64,768]{1,0:T(8,128)(2,1)}, u32[]{:S(2)}) copy-start(bf16[64,768]{1,0:T(8,128)(2,1)} %refs_5_.1) | copy-start | bytes 294916
  6.9 0.9 %copy-start.6 = (bf16[64,768]{1,0:T(8,128)(2,1)S(1)}, bf16[64,768]{1,0:T(8,128)(2,1)}, u32[]{:S(2)}) copy-start(bf16[64,768]{1,0:T(8,128)(2,1)} %refs_6_.1) | copy-start | bytes 294916
  7.8 0.9 %copy-start.7 = (bf16[64,768]{1,0:T(8,128)(2,1)S(1)}, bf16[64,768]{1,0:T(8,128)(2,1)}, u32[]{:S(2)}) copy-start(bf16[64,768]{1,0:T(8,128)(2,1)} %refs_7_.1) | copy-start | bytes 294916

commit v2 on v1

--- a/solution.py
+++ b/solution.py
@@ -40,7 +40,7 @@
 
 def kernel(blocks, vrows, arows, heads, *refs):
     (vq, vk, vv, vc, aq, ak, av, ac, inter, out) = refs[:10]
-    (vid, win, e_on, dp_on, e_far, dp_far, p1, ds1, p2, ds2, own, s_near, s_far, r_near, r_far,
+    (spans, vid, win, e_on, dp_on, e_far, dp_far, p1, ds1, p2, ds2, own, s_near, s_far, r_near, r_far,
      es, ls, re_n, re_f, re_fn, rl_f, rl_nf, fac_on, fac_far, bias,
      load_sem, near_sem, far_ssem, far_rsem, es_ssem, es_rsem, ls_ssem, ls_rsem,
      kv_ssem, kv_rsem, oq_ssem, oq_rsem, nr_ssem, nr_rsem) = refs[10:]
@@ -73,6 +73,8 @@
     def _():
         pl.semaphore_signal(barrier, inc=1, device_id=here(nf), device_id_type=MESH)
 
+    span_load = pltpu.make_async_copy(inter, spans, load_sem.at[8])
+    span_load.start()
     loads = []
     for t, ref in enumerate((aq, ak, av, ac)):
         loads.append(pltpu.make_async_copy(ref, win.at[t, pl.ds(0, arows)], load_sem.at[t]))
@@ -81,7 +83,8 @@
     for copy in loads:
         copy.start()
 
-    first, last = inter[b, 0], inter[b, 1]
+    span_load.wait()
+    first, last = spans[0, b], spans[1, b]
     lane = lax.broadcasted_iota(jnp.int32, (1, DH), 1)
     rows_on = jnp.where(lane < arows, b * arows + lane, n * arows + lane - arows)
     mask_on = (rows_on >= first) & (rows_on < last)
@@ -374,6 +377,7 @@
     dma = pltpu.SemaphoreType.DMA
     audio = (4, arows, features)
     scratch = [
+        pltpu.SMEM((2, blocks), jnp.int32),
         pltpu.VMEM((4, vrows, features), BF16),
         pltpu.VMEM((4, 3 * arows, features), BF16),
         pltpu.VMEM((heads, vrows, 2 * arows), F32),
@@ -392,7 +396,7 @@
         *[pltpu.VMEM((3, 8, DH), F32)] * 7,
         *[pltpu.VMEM((2, 8, DH), F32)] * 2,
         pltpu.VMEM((3 * arows, DH), F32),
-        dma((8,)),
+        dma((9,)),
         dma((2,)),
         dma((CHUNKS,)),
         dma((CHUNKS,)),
@@ -408,10 +412,11 @@
         dma((2,)),
     ]
     any_space = pl.BlockSpec(memory_space=pl.ANY)
+    in_hbm = pl.BlockSpec(memory_space=pltpu.HBM)
     joint = pl.pallas_call(
         functools.partial(kernel, blocks, vrows, arows, heads),
         out_shape=pltpu.VMEM((sum(sizes), features), BF16),
-        in_specs=[any_space] * 8 + [pl.BlockSpec(memory_space=pltpu.SMEM)],
+        in_specs=[in_hbm] * 9,
         out_specs=pl.BlockSpec(memory_space=pltpu.VMEM),
         scratch_shapes=scratch,
         compiler_params=pltpu.CompilerParams(
@@ -421,7 +426,7 @@
             flops=24 * heads * vrows * 3 * arows * DH, bytes_accessed=12 * (vrows + arows) * features, transcendentals=0
         ),
         name="cross_attention",
-    )(video_query, video_key, video_value, video_cot, audio_query, audio_key, audio_value, audio_cot, intersection)
+    )(*[pltpu.with_memory_space_constraint(x, pltpu.HBM) for x in (video_query, video_key, video_value, video_cot, audio_query, audio_key, audio_value, audio_cot, jnp.transpose(intersection))])
     joint = pltpu.with_memory_space_constraint(joint, pltpu.VMEM)
     return tuple(
         pl.pallas_call(

time: 32.2 us -> 23.2 us (0.72)
  local copies, waits for them, and re-layouts: 8.03 us -> 0 us
  Pallas kernels: 23.2 us -> 22.4 us
    unnamed x17 -> x0, local copies, waits for them, and re-layouts: 8.03 us -> none
    pallas_call x1, Pallas kernels: 22.1 us -> 21.3 us  [local(): pl.pallas_call(functools.partial(kernel, blocks, vrows, arows, heads), ou...]
where the time goes in v2:
time: 23.2 us; the launch traced here: 23 us
  Pallas kernels  22.4 us (97%)
  between operations  0.64 us (3%)
    pallas_call x1, Pallas kernels, local(): pl.pallas_call(functools.partial(kernel, blocks, vrows, arows, heads), ou...  21.3 us
    pallas_call x1, Pallas kernels, local(): pl.pallas_call(functools.partial(spread, sizes), out_shape=[jax.ShapeDtyp...  1.07 us

profile of v2, /device:TPU:1, one launch (start us, length us, event | category | flops | bytes accessed | tf_op | source)
XLA Modules:
  0.0 23.0 jit_solution(4088912419571731677)
XLA Ops:
  0.6 21.3 %cross_attention.1.joint = bf16[768,768]{1,0:T(8,128)(2,1)S(1)} custom-call(bf16[128,768]{1,0:T(8,128)(2,1)} %refs_0_.1, bf16[128,768]{1,0:T(8,128)(2,1)} %refs_1_.1, bf16[128,768]{1,0:T(8,128)(2,1)} %refs_2_.1, bf16[128,768]{1,0:T(8,128)(2,1)} %refs_3_.1, bf16[64,768]{1,0:T(8,128)(2,1)} %refs_4_.1, bf16[64,768]{1,0:T(8,128)(2,1)} %refs_5_.1, ...), custom_call_target="tpu_custom_call" | custom-call | flops 452984832 | bytes 1769472 | tf_op jit(solution)/shard_map/cross_attention/pallas_call | solution.py:416
  22.0 1.1 %spread.1 = (bf16[128,768]{1,0:T(8,128)(2,1)}, bf16[64,768]{1,0:T(8,128)(2,1)}, bf16[128,768]{1,0:T(8,128)(2,1)}, bf16[128,768]{1,0:T(8,128)(2,1)}, bf16[128,768...) custom-call(bf16[768,768]{1,0:T(8,128)(2,1)S(1)} %cross_attention.1.joint), custom_call_target="tpu_custom_call" | custom-call | tf_op jit(solution)/shard_map/spread/pallas_call | solution.py:432

commit v3 on v2

v3 whole, which is shorter than its diff:
```python
import functools

import jax
import jax.numpy as jnp
from jax import lax
from jax.experimental import pallas as pl
from jax.experimental.pallas import tpu as pltpu
from jax.sharding import PartitionSpec as P

DH = 128
NEG = -1e30
ABSENT = -2e30
LOG2E = 1.4426950408889634
MESH = pl.DeviceIdType.MESH
F32 = jnp.float32
BF16 = jnp.bfloat16
Q, K, V, C = 0, 1, 2, 3
DK, DV, OUT, DQ = 0, 1, 2, 3
FIRST = ((K, 1), (V, 1), (Q, 0), (C, 0), (Q, 1), (C, 1))
LATER = ((Q, 2), (C, 2), (K, 2), (V, 2))


def dot_nt(a, b):
    return lax.dot_general(a, b, (((1,), (1,)), ((), ())), preferred_element_type=F32)


def dot_nn(a, b):
    return lax.dot_general(a, b, (((1,), (0,)), ((), ())), preferred_element_type=F32)


def dot_tn(a, b):
    return lax.dot_general(a, b, (((0,), (0,)), ((), ())), preferred_element_type=F32)


def joined(top_here, parts):
    top = functools.reduce(jnp.maximum, [p[0] for p in parts])
    shares = [jnp.exp2(p[0] - top) for p in parts]
    inverse = 1.0 / sum(shares)
    return jnp.exp2(top_here - top) * inverse, sum(w * p[1] for w, p in zip(shares, parts)) * inverse


def kernel(blocks, vrows, arows, heads, *refs):
    (vq, vk, vv, vc, aq, ak, av, ac, inter, out) = refs[:10]
    (spans, vqc, vkv, qc, win, qb, e_on, dp_on, e_far, dp_far, p1, ds1, p2, ds2, own_a, own_v,
     s_near, r_near, s_video, r_video, s_far, r_far, es, ls, re_f, rl_f, m_on, m_far, bias,
     load_sem, near_ssem, near_rsem, far_ssem, far_rsem, st_ssem, st_rsem,
     kv_ssem, kv_rsem, oq_ssem, oq_rsem, nr_ssem, nr_rsem) = refs[10:]
    scale = DH ** (-0.5)
    scale2 = scale * LOG2E
    two = 2 * arows
    three = 3 * arows
    pairs = heads // 2
    wide = 2 * DH

    b = lax.axis_index("video")
    odd = lax.rem(b, 2)
    n = b + 1 - 2 * odd
    f = b - 1 + 2 * odd
    has_f = (f >= 0) & (f < blocks)

    def here(index):
        return {"video": index}

    barrier = pltpu.get_barrier_semaphore()

    @pl.when(has_f)
    def _():
        pl.semaphore_signal(barrier, inc=1, device_id=here(f), device_id_type=MESH)

    pl.semaphore_signal(barrier, inc=1, device_id=here(n), device_id_type=MESH)

    span_load = pltpu.make_async_copy(inter, spans, load_sem.at[8])
    loads = [
        pltpu.make_async_copy(vk, vkv.at[0, pl.ds(0, vrows)], load_sem.at[0]),
        pltpu.make_async_copy(vv, vkv.at[1, pl.ds(0, vrows)], load_sem.at[1]),
        pltpu.make_async_copy(aq, qc.at[0, pl.ds(0, arows)], load_sem.at[2]),
        pltpu.make_async_copy(ac, qc.at[1, pl.ds(0, arows)], load_sem.at[3]),
        pltpu.make_async_copy(ak, win.at[0, pl.ds(0, arows)], load_sem.at[4]),
        pltpu.make_async_copy(av, win.at[1, pl.ds(0, arows)], load_sem.at[5]),
        pltpu.make_async_copy(vq, vqc.at[0], load_sem.at[6]),
        pltpu.make_async_copy(vc, vqc.at[1], load_sem.at[7]),
    ]
    for copy in (span_load, *loads):
        copy.start()

    def remote(src, dst, ssem, rsem, device):
        return pltpu.make_async_remote_copy(
            src_ref=src, dst_ref=dst, send_sem=ssem, recv_sem=rsem, device_id=here(device), device_id_type=MESH
        )

    def pair_cols(p):
        return pl.ds(p * wide, wide)

    def head_cols(h):
        return pl.ds(h * DH, DH)

    near_in = [
        remote(ref, dst, near_ssem.at[t], near_rsem.at[t], n)
        for t, (ref, dst) in enumerate((
            (vk, vkv.at[0, pl.ds(vrows, vrows)]),
            (vv, vkv.at[1, pl.ds(vrows, vrows)]),
            (ak, win.at[0, pl.ds(arows, arows)]),
            (av, win.at[1, pl.ds(arows, arows)]),
        ))
    ]
    far_in = [
        [remote(ref.at[:, pair_cols(p)], dst.at[:, pair_cols(p)], far_ssem.at[t, p], far_rsem.at[t, p], f)
         for p in range(pairs)]
        for t, (ref, dst) in enumerate((
            (aq, qc.at[0, pl.ds(arows, arows)]),
            (ak, win.at[0, pl.ds(two, arows)]),
            (av, win.at[1, pl.ds(two, arows)]),
            (ac, qc.at[1, pl.ds(arows, arows)]),
        ))
    ]
    es_f = remote(es, re_f, st_ssem.at[0], st_rsem.at[0], f)
    ls_f = remote(ls, rl_f, st_ssem.at[1], st_rsem.at[1], f)
    kv_far = [
        remote(s_far.at[pl.ds(0, 2), :, pair_cols(p)], r_far.at[pl.ds(0, 2), :, pair_cols(p)],
               kv_ssem.at[p], kv_rsem.at[p], f)
        for p in range(pairs)
    ]
    oq_far = [
        remote(s_far.at[pl.ds(2, 2), :, pair_cols(p)], r_far.at[pl.ds(2, 2), :, pair_cols(p)],
               oq_ssem.at[p], oq_rsem.at[p], f)
        for p in range(pairs)
    ]
    kv_near = remote(s_near, r_near, nr_ssem.at[pairs], nr_rsem.at[pairs], n)
    kv_video = [
        remote(s_video.at[:, :, pair_cols(p)], r_video.at[:, :, pair_cols(p)], nr_ssem.at[p], nr_rsem.at[p], n)
        for p in range(pairs)
    ]

    for p in range(pairs):
        for t in range(2):
            for half in range(2):
                rows = pl.ds(half * two, two)
                qb[t, p, rows, :] = jnp.zeros((two, wide), BF16)

    for ref in (es, ls, m_on, m_far):
        ref[...] = jnp.zeros_like(ref)

    pl.semaphore_wait(barrier, 1 + has_f.astype(jnp.int32))

    @pl.when(has_f)
    def _():
        far_in[K][0].start()
        far_in[V][0].start()

    for copy in near_in:
        copy.start()

    @pl.when(has_f)
    def _():
        for t, p in FIRST:
            far_in[t][p].start()

    span_load.wait()
    first, last = spans[0, b], spans[1, b]
    lane = lax.broadcasted_iota(jnp.int32, (1, two), 1)
    lane = jnp.where(lane < arows, lane, lane - arows)
    mask_far = (f * arows + lane >= first) & (f * arows + lane < last)
    mask_near = (b * arows + lane >= spans[0, n]) & (b * arows + lane < spans[1, n])
    bias_near = jnp.where(mask_near, 0.0, NEG)
    sub = lax.broadcasted_iota(jnp.int32, (three, vrows), 0)
    rows_sub = jnp.where(sub < arows, b * arows + sub,
                         jnp.where(sub < two, n * arows + sub - arows, f * arows + sub - two))
    bias[...] = jnp.where((rows_sub >= first) & (rows_sub < last), 0.0, NEG)

    @pl.when(jnp.logical_not(has_f))
    def _():
        for t in range(2):
            win[t, pl.ds(two, arows), :] = jnp.zeros((arows, heads * DH), BF16)
            qc[t, pl.ds(arows, arows), :] = jnp.zeros((arows, heads * DH), BF16)
        for t in range(4):
            r_far[t] = jnp.zeros((arows, heads * DH), BF16)
        for ref in (re_f, rl_f):
            ref[0] = jnp.full(ref.shape[1:], NEG, F32)
            ref[1] = jnp.zeros(ref.shape[1:], F32)

    for copy in loads:
        copy.wait()

    def place_blocks(p, start):
        for t in range(2):
            for k in range(2):
                qb[t, p, pl.ds(2 * start + k * arows, arows), head_cols(k)] = (
                    qc[t, pl.ds(start, arows), head_cols(2 * p + k)]
                )

    for p in range(pairs):
        place_blocks(p, 0)

    near_in[0].wait_recv()
    near_in[1].wait_recv()

    for p in range(pairs):
        s = dot_nt(vkv[0, :, pair_cols(p)], qb[0, p, pl.ds(0, two), :]) * scale2
        dp = dot_nt(vkv[1, :, pair_cols(p)], qb[1, p, pl.ds(0, two), :])
        s = jnp.concatenate([s[:vrows], s[vrows:] + bias_near], axis=0)
        top = jnp.max(s, axis=0, keepdims=True)
        e = jnp.exp2(s - top)
        e_on[p] = e
        dp_on[p] = dp
        total = jnp.sum(e, axis=0, keepdims=True)
        m_on[pl.ds(p, 1), :] = top
        es[0, pl.ds(p, 1), :] = top + jnp.log(total) * LOG2E
        es[1, pl.ds(p, 1), :] = jnp.sum(e * dp, axis=0, keepdims=True) / total

    @pl.when(has_f)
    def _():
        es_f.start()
        for t, p in LATER:
            far_in[t][p].start()

    near_in[2].wait_recv()
    near_in[3].wait_recv()

    def stage_scores(p):
        @pl.when(has_f)
        def _():
            far_in[K][p].wait_recv()
            far_in[V][p].wait_recv()

        for h in (2 * p, 2 * p + 1):
            cols = head_cols(h)
            qv, cv = vqc[0, :, cols], vqc[1, :, cols]
            s = dot_nt(win[0, :, cols], qv) * scale2 + bias[...]
            dp = dot_nt(win[1, :, cols], cv)
            top = jnp.max(s, axis=0, keepdims=True)
            e = jnp.exp2(s - top)
            inverse = 1.0 / jnp.sum(e, axis=0, keepdims=True)
            prob = e * inverse
            delta = jnp.sum(prob * dp, axis=0, keepdims=True)
            weights = prob.astype(BF16)
            dscore = (prob * (dp - delta)).astype(BF16)
            p1[h] = weights
            ds1[h] = dscore
            s_far[DK, :, cols] = (dot_nn(dscore[two:], qv) * scale).astype(BF16)
            s_far[DV, :, cols] = dot_nn(weights[two:], cv).astype(BF16)

        @pl.when(has_f)
        def _():
            kv_far[p].start()

    def stage_terms(p):
        @pl.when(has_f)
        def _():
            far_in[Q][p].wait_recv()
            far_in[C][p].wait_recv()

        place_blocks(p, arows)
        s = dot_nt(vkv[0, pl.ds(0, vrows), pair_cols(p)], qb[0, p, pl.ds(two, two), :]) * scale2
        dp = dot_nt(vkv[1, pl.ds(0, vrows), pair_cols(p)], qb[1, p, pl.ds(two, two), :])
        top = jnp.max(s, axis=0, keepdims=True)
        e = jnp.exp2(s - top)
        e_far[p] = e
        dp_far[p] = dp
        total = jnp.sum(e, axis=0, keepdims=True)
        m_far[pl.ds(p, 1), :] = jnp.where(mask_far, top, ABSENT)
        ls[0, pl.ds(p, 1), :] = jnp.where(mask_far, top + jnp.log(total) * LOG2E, NEG)
        ls[1, pl.ds(p, 1), :] = jnp.where(mask_far, jnp.sum(e * dp, axis=0, keepdims=True) / total, 0.0)

    def terms_of(ref, p):
        return [ref[0, pl.ds(p, 1), :], ref[1, pl.ds(p, 1), :]]

    def stage_far(p):
        factor, delta = joined(m_far[pl.ds(p, 1), :], [terms_of(ls, p), terms_of(re_f, p)])
        prob = e_far[p] * factor
        weights = prob.astype(BF16)
        dscore = (prob * (dp_far[p] - delta)).astype(BF16)
        p2[p, :, pl.ds(two, two)] = weights
        ds2[p, :, pl.ds(two, two)] = dscore
        weights, dscore = weights.T, dscore.T
        for k in range(2):
            cols = head_cols(2 * p + k)
            rows = slice(k * arows, (k + 1) * arows)
            s_far[OUT, :, cols] = dot_nn(weights[rows], vkv[1, pl.ds(0, vrows), cols]).astype(BF16)
            s_far[DQ, :, cols] = (dot_nn(dscore[rows], vkv[0, pl.ds(0, vrows), cols]) * scale).astype(BF16)

        @pl.when(has_f)
        def _():
            oq_far[p].start()

    stage_scores(0)
    stage_scores(1)
    stage_terms(0)

    @pl.when(has_f)
    def _():
        es_f.wait_recv()

    stage_far(0)
    stage_terms(1)
    stage_terms(2)

    @pl.when(has_f)
    def _():
        ls_f.start()

    stage_far(1)
    stage_far(2)
    stage_scores(2)

    for h in range(heads):
        cols = head_cols(h)
        dk = dot_nn(ds1[h, pl.ds(0, two), :], vqc[0, :, cols]) * scale
        dv = dot_nn(p1[h, pl.ds(0, two), :], vqc[1, :, cols])
        own_a[DK, :, cols] = dk[:arows]
        own_a[DV, :, cols] = dv[:arows]
        s_near[DK, :, cols] = dk[arows:].astype(BF16)
        s_near[DV, :, cols] = dv[arows:].astype(BF16)
    kv_near.start()

    def place(index):
        starts = [0, vrows, vrows + arows, 2 * vrows + arows, 3 * vrows + arows,
                  4 * vrows + arows, 4 * vrows + 2 * arows, 4 * vrows + 3 * arows]
        return pl.ds(starts[index], arows if index in (1, 5, 6, 7) else vrows)

    for h in range(heads):
        cols = head_cols(h)
        out[place(0), cols] = dot_tn(p1[h], win[1, :, cols]).astype(BF16)
        out[place(2), cols] = (dot_tn(ds1[h], win[0, :, cols]) * scale).astype(BF16)

    @pl.when(has_f)
    def _():
        ls_f.wait_recv()

    for p in range(pairs):
        factor, delta = joined(m_on[pl.ds(p, 1), :], [terms_of(es, p), terms_of(rl_f, p)])
        prob = e_on[p] * factor
        weights = prob.astype(BF16)
        dscore = (prob * (dp_on[p] - delta)).astype(BF16)
        s_video[0, :, pair_cols(p)] = (dot_nn(dscore[vrows:], qb[0, p, pl.ds(0, two), :]) * scale).astype(BF16)
        s_video[1, :, pair_cols(p)] = dot_nn(weights[vrows:], qb[1, p, pl.ds(0, two), :]).astype(BF16)
        kv_video[p].start()
        p2[p, :, pl.ds(0, two)] = weights[:vrows]
        ds2[p, :, pl.ds(0, two)] = dscore[:vrows]
        weights, dscore = weights.T, dscore.T
        for k in range(2):
            cols = head_cols(2 * p + k)
            rows = slice(k * arows, (k + 1) * arows)
            own_a[OUT, :, cols] = dot_nn(weights[rows], vkv[1, :, cols])
            own_a[DQ, :, cols] = dot_nn(dscore[rows], vkv[0, :, cols]) * scale

    for p in range(pairs):
        own_v[0, :, pair_cols(p)] = dot_nn(ds2[p], qb[0, p]) * scale
        own_v[1, :, pair_cols(p)] = dot_nn(p2[p], qb[1, p])

    for copy in near_in:
        copy.wait_send()

    @pl.when(has_f)
    def _():
        for copy in (*far_in[Q], *far_in[K], *far_in[V], *far_in[C], es_f):
            copy.wait_send()

    kv_near.wait_recv()
    for pair, copies, p in (
        ((DK, DV), kv_far, 0), ((DK, DV), kv_far, 1), ((OUT, DQ), oq_far, 0),
        ((OUT, DQ), oq_far, 1), ((OUT, DQ), oq_far, 2), ((DK, DV), kv_far, 2),
    ):
        @pl.when(has_f)
        def _(copy=copies[p]):
            copy.wait_recv()

        for t in pair:
            cols = pair_cols(p)
            total = own_a[t, :, cols] + r_far[t, :, cols].astype(F32)
            if t in (DK, DV):
                total += r_near[t, :, cols].astype(F32)
            out[place({OUT: 1, DQ: 5, DK: 6, DV: 7}[t]), cols] = total.astype(BF16)
    for p in range(pairs):
        kv_video[p].wait_recv()
        for t in range(2):
            cols = pair_cols(p)
            out[place(3 + t), cols] = (own_v[t, :, cols] + r_video[t, :, cols].astype(F32)).astype(BF16)

    for copy in (kv_near, *kv_video):
        copy.wait_send()

    @pl.when(has_f)
    def _():
        for copy in (*kv_far, *oq_far, ls_f):
            copy.wait_send()


def spread(sizes, joint, *refs):
    outs, sems = refs[: len(sizes)], refs[len(sizes)]
    start, copies = 0, []
    for index, size in enumerate(sizes):
        copies.append(pltpu.make_async_copy(joint.at[pl.ds(start, size)], outs[index], sems.at[index]))
        start += size
    for copy in copies:
        copy.start()
    for copy in copies:
        copy.wait()


def local(video_query, video_key, video_value, video_cot, audio_query, audio_key, audio_value, audio_cot, intersection):
    vrows, features = video_query.shape
    arows = audio_query.shape[0]
    heads = features // DH
    blocks = lax.axis_size("video")
    sizes = [vrows, arows, vrows, vrows, vrows, arows, arows, arows]
    dma = pltpu.SemaphoreType.DMA
    pairs = heads // 2
    two, three, wide = 2 * arows, 3 * arows, 2 * DH
    scratch = [
        pltpu.SMEM((2, blocks), jnp.int32),
        pltpu.VMEM((2, vrows, features), BF16),
        pltpu.VMEM((2, 2 * vrows, features), BF16),
        pltpu.VMEM((2, two, features), BF16),
        pltpu.VMEM((2, three, features), BF16),
        pltpu.VMEM((2, pairs, 2 * two, wide), BF16),
        *[pltpu.VMEM((pairs, 2 * vrows, two), F32)] * 2,
        *[pltpu.VMEM((pairs, vrows, two), F32)] * 2,
        *[pltpu.VMEM((heads, three, vrows), BF16)] * 2,
        *[pltpu.VMEM((pairs, vrows, 2 * two), BF16)] * 2,
        pltpu.VMEM((4, arows, features), F32),
        pltpu.VMEM((2, vrows, features), F32),
        *[pltpu.VMEM((2, arows, features), BF16)] * 2,
        *[pltpu.VMEM((2, vrows, features), BF16)] * 2,
        *[pltpu.VMEM((4, arows, features), BF16)] * 2,
        *[pltpu.VMEM((2, 4, two), F32)] * 4,
        *[pltpu.VMEM((4, two), F32)] * 2,
        pltpu.VMEM((three, vrows), F32),
        dma((9,)),
        *[dma((4,))] * 2,
        *[dma((4, pairs))] * 2,
        *[dma((2,))] * 2,
        *[dma((pairs,))] * 4,
        *[dma((1 + pairs,))] * 2,
    ]
    any_space = pl.BlockSpec(memory_space=pl.ANY)
    in_hbm = pl.BlockSpec(memory_space=pltpu.HBM)
    joint = pl.pallas_call(
        functools.partial(kernel, blocks, vrows, arows, heads),
        out_shape=pltpu.VMEM((sum(sizes), features), BF16),
        in_specs=[in_hbm] * 9,
        out_specs=pl.BlockSpec(memory_space=pltpu.VMEM),
        scratch_shapes=scratch,
        compiler_params=pltpu.CompilerParams(
            collective_id=0, has_side_effects=True, vmem_limit_bytes=24 * 1024 * 1024
        ),
        cost_estimate=pl.CostEstimate(
            flops=24 * heads * vrows * 3 * arows * DH, bytes_accessed=12 * (vrows + arows) * features, transcendentals=0
        ),
        name="cross_attention",
    )(*[pltpu.with_memory_space_constraint(x, pltpu.HBM) for x in (video_query, video_key, video_value, video_cot, audio_query, audio_key, audio_value, audio_cot, jnp.transpose(intersection))])
    joint = pltpu.with_memory_space_constraint(joint, pltpu.VMEM)
    return tuple(
        pl.pallas_call(
            functools.partial(spread, sizes),
            out_shape=[jax.ShapeDtypeStruct((size, features), BF16) for size in sizes],
            in_specs=[any_space],
            out_specs=[any_space] * len(sizes),
            scratch_shapes=[dma((len(sizes),))],
            name="spread",
        )(joint)
    )


def solution(mesh):
    rows = P(("clip", "video"), "audio")
    return jax.shard_map(
        local,
        mesh=mesh,
        in_specs=(rows,) * 8 + (P("clip", None),),
        out_specs=(rows,) * 8,
        check_vma=False,
    )
```

time: 23.2 us -> 20.7 us (0.89)
  Pallas kernels: 22.4 us -> 19.9 us
    pallas_call x1, Pallas kernels: 21.3 us -> 18.9 us  [local(): pl.pallas_call(functools.partial(kernel, blocks, vrows, arows, heads), ou...]
where the time goes in v3:
time: 20.7 us; the launch traced here: 20.6 us
  Pallas kernels  19.9 us (96%)
  between operations  0.64 us (3%)
    pallas_call x1, Pallas kernels, local(): pl.pallas_call(functools.partial(kernel, blocks, vrows, arows, heads), ou...  18.9 us
    pallas_call x1, Pallas kernels, local(): pl.pallas_call(functools.partial(spread, sizes), out_shape=[jax.ShapeDtyp...  1.07 us

profile of v3, /device:TPU:1, one launch (start us, length us, event | category | flops | bytes accessed | tf_op | source)
XLA Modules:
  0.0 20.6 jit_solution(9046657993786156284)
XLA Ops:
  0.6 18.9 %cross_attention.1.joint = bf16[768,768]{1,0:T(8,128)(2,1)S(1)} custom-call(bf16[128,768]{1,0:T(8,128)(2,1)} %refs_0_.1, bf16[128,768]{1,0:T(8,128)(2,1)} %refs_1_.1, bf16[128,768]{1,0:T(8,128)(2,1)} %refs_2_.1, bf16[128,768]{1,0:T(8,128)(2,1)} %refs_3_.1, bf16[64,768]{1,0:T(8,128)(2,1)} %refs_4_.1, bf16[64,768]{1,0:T(8,128)(2,1)} %refs_5_.1, ...), custom_call_target="tpu_custom_call" | custom-call | flops 452984832 | bytes 1769472 | tf_op jit(solution)/shard_map/cross_attention/pallas_call | solution.py:437
  19.5 1.1 %spread.1 = (bf16[128,768]{1,0:T(8,128)(2,1)}, bf16[64,768]{1,0:T(8,128)(2,1)}, bf16[128,768]{1,0:T(8,128)(2,1)}, bf16[128,768]{1,0:T(8,128)(2,1)}, bf16[128,768...) custom-call(bf16[768,768]{1,0:T(8,128)(2,1)S(1)} %cross_attention.1.joint), custom_call_target="tpu_custom_call" | custom-call | tf_op jit(solution)/shard_map/spread/pallas_call | solution.py:453

commit v4 on v3

--- a/solution.py
+++ b/solution.py
@@ -43,8 +43,7 @@
     (vq, vk, vv, vc, aq, ak, av, ac, inter, out) = refs[:10]
     (spans, vqc, vkv, qc, win, qb, e_on, dp_on, e_far, dp_far, p1, ds1, p2, ds2, own_a, own_v,
      s_near, r_near, s_video, r_video, s_far, r_far, es, ls, re_f, rl_f, m_on, m_far, bias,
-     load_sem, near_ssem, near_rsem, far_ssem, far_rsem, st_ssem, st_rsem,
-     kv_ssem, kv_rsem, oq_ssem, oq_rsem, nr_ssem, nr_rsem) = refs[10:]
+     load_sem, near_sem, far_sem, terms_sem, kv_sem, oq_sem, back_sem, sent) = refs[10:]
     scale = DH ** (-0.5)
     scale2 = scale * LOG2E
     two = 2 * arows
@@ -69,16 +68,16 @@
 
     pl.semaphore_signal(barrier, inc=1, device_id=here(n), device_id_type=MESH)
 
-    span_load = pltpu.make_async_copy(inter, spans, load_sem.at[8])
+    span_load = pltpu.make_async_copy(inter, spans, load_sem.at[4])
     loads = [
         pltpu.make_async_copy(vk, vkv.at[0, pl.ds(0, vrows)], load_sem.at[0]),
-        pltpu.make_async_copy(vv, vkv.at[1, pl.ds(0, vrows)], load_sem.at[1]),
-        pltpu.make_async_copy(aq, qc.at[0, pl.ds(0, arows)], load_sem.at[2]),
-        pltpu.make_async_copy(ac, qc.at[1, pl.ds(0, arows)], load_sem.at[3]),
-        pltpu.make_async_copy(ak, win.at[0, pl.ds(0, arows)], load_sem.at[4]),
-        pltpu.make_async_copy(av, win.at[1, pl.ds(0, arows)], load_sem.at[5]),
-        pltpu.make_async_copy(vq, vqc.at[0], load_sem.at[6]),
-        pltpu.make_async_copy(vc, vqc.at[1], load_sem.at[7]),
+        pltpu.make_async_copy(vv, vkv.at[1, pl.ds(0, vrows)], load_sem.at[0]),
+        pltpu.make_async_copy(aq, qc.at[0, pl.ds(0, arows)], load_sem.at[1]),
+        pltpu.make_async_copy(ac, qc.at[1, pl.ds(0, arows)], load_sem.at[1]),
+        pltpu.make_async_copy(ak, win.at[0, pl.ds(0, arows)], load_sem.at[2]),
+        pltpu.make_async_copy(av, win.at[1, pl.ds(0, arows)], load_sem.at[2]),
+        pltpu.make_async_copy(vq, vqc.at[0], load_sem.at[3]),
+        pltpu.make_async_copy(vc, vqc.at[1], load_sem.at[3]),
     ]
     for copy in (span_load, *loads):
         copy.start()
@@ -88,14 +87,18 @@
             src_ref=src, dst_ref=dst, send_sem=ssem, recv_sem=rsem, device_id=here(device), device_id_type=MESH
         )
 
+    def wait_for(ref, sem):
+        pltpu.make_async_copy(ref, ref, sem).wait()
+
     def pair_cols(p):
         return pl.ds(p * wide, wide)
 
     def head_cols(h):
         return pl.ds(h * DH, DH)
 
+    to_n, to_f = sent.at[0], sent.at[1]
     near_in = [
-        remote(ref, dst, near_ssem.at[t], near_rsem.at[t], n)
+        remote(ref, dst, to_n, near_sem.at[t // 2], n)
         for t, (ref, dst) in enumerate((
             (vk, vkv.at[0, pl.ds(vrows, vrows)]),
             (vv, vkv.at[1, pl.ds(vrows, vrows)]),
@@ -104,30 +107,27 @@
         ))
     ]
     far_in = [
-        [remote(ref.at[:, pair_cols(p)], dst.at[:, pair_cols(p)], far_ssem.at[t, p], far_rsem.at[t, p], f)
-         for p in range(pairs)]
-        for t, (ref, dst) in enumerate((
-            (aq, qc.at[0, pl.ds(arows, arows)]),
-            (ak, win.at[0, pl.ds(two, arows)]),
-            (av, win.at[1, pl.ds(two, arows)]),
-            (ac, qc.at[1, pl.ds(arows, arows)]),
-        ))
-    ]
-    es_f = remote(es, re_f, st_ssem.at[0], st_rsem.at[0], f)
-    ls_f = remote(ls, rl_f, st_ssem.at[1], st_rsem.at[1], f)
+        [remote(ref.at[:, pair_cols(p)], dst.at[:, pair_cols(p)], to_f, far_sem.at[kind, p], f) for p in range(pairs)]
+        for ref, dst, kind in (
+            (aq, qc.at[0, pl.ds(arows, arows)], 0),
+            (ak, win.at[0, pl.ds(two, arows)], 1),
+            (av, win.at[1, pl.ds(two, arows)], 1),
+            (ac, qc.at[1, pl.ds(arows, arows)], 0),
+        )
+    ]
+    es_f = remote(es, re_f, sent.at[2], terms_sem.at[0], f)
+    ls_f = remote(ls, rl_f, sent.at[3], terms_sem.at[1], f)
     kv_far = [
-        remote(s_far.at[pl.ds(0, 2), :, pair_cols(p)], r_far.at[pl.ds(0, 2), :, pair_cols(p)],
-               kv_ssem.at[p], kv_rsem.at[p], f)
+        remote(s_far.at[pl.ds(0, 2), :, pair_cols(p)], r_far.at[pl.ds(0, 2), :, pair_cols(p)], to_f, kv_sem.at[p], f)
         for p in range(pairs)
     ]
     oq_far = [
-        remote(s_far.at[pl.ds(2, 2), :, pair_cols(p)], r_far.at[pl.ds(2, 2), :, pair_cols(p)],
-               oq_ssem.at[p], oq_rsem.at[p], f)
+        remote(s_far.at[pl.ds(2, 2), :, pair_cols(p)], r_far.at[pl.ds(2, 2), :, pair_cols(p)], to_f, oq_sem.at[p], f)
         for p in range(pairs)
     ]
-    kv_near = remote(s_near, r_near, nr_ssem.at[pairs], nr_rsem.at[pairs], n)
+    kv_near = remote(s_near, r_near, to_n, back_sem.at[pairs], n)
     kv_video = [
-        remote(s_video.at[:, :, pair_cols(p)], r_video.at[:, :, pair_cols(p)], nr_ssem.at[p], nr_rsem.at[p], n)
+        remote(s_video.at[:, :, pair_cols(p)], r_video.at[:, :, pair_cols(p)], to_n, back_sem.at[p], n)
         for p in range(pairs)
     ]
 
@@ -178,8 +178,10 @@
             ref[0] = jnp.full(ref.shape[1:], NEG, F32)
             ref[1] = jnp.zeros(ref.shape[1:], F32)
 
-    for copy in loads:
-        copy.wait()
+    wait_for(vkv.at[:, pl.ds(0, vrows)], load_sem.at[0])
+    wait_for(qc.at[:, pl.ds(0, arows)], load_sem.at[1])
+    wait_for(win.at[:, pl.ds(0, arows)], load_sem.at[2])
+    wait_for(vqc, load_sem.at[3])
 
     def place_blocks(p, start):
         for t in range(2):
@@ -191,8 +193,7 @@
     for p in range(pairs):
         place_blocks(p, 0)
 
-    near_in[0].wait_recv()
-    near_in[1].wait_recv()
+    wait_for(vkv.at[:, pl.ds(vrows, vrows)], near_sem.at[0])
 
     for p in range(pairs):
         s = dot_nt(vkv[0, :, pair_cols(p)], qb[0, p, pl.ds(0, two), :]) * scale2
@@ -213,14 +214,12 @@
         for t, p in LATER:
             far_in[t][p].start()
 
-    near_in[2].wait_recv()
-    near_in[3].wait_recv()
+    wait_for(win.at[:, pl.ds(arows, arows)], near_sem.at[1])
 
     def stage_scores(p):
         @pl.when(has_f)
         def _():
-            far_in[K][p].wait_recv()
-            far_in[V][p].wait_recv()
+            wait_for(win.at[:, pl.ds(two, arows), pair_cols(p)], far_sem.at[1, p])
 
         for h in (2 * p, 2 * p + 1):
             cols = head_cols(h)
@@ -246,8 +245,7 @@
     def stage_terms(p):
         @pl.when(has_f)
         def _():
-            far_in[Q][p].wait_recv()
-            far_in[C][p].wait_recv()
+            wait_for(qc.at[:, pl.ds(arows, arows), pair_cols(p)], far_sem.at[0, p])
 
         place_blocks(p, arows)
         s = dot_nt(vkv[0, pl.ds(0, vrows), pair_cols(p)], qb[0, p, pl.ds(two, two), :]) * scale2
@@ -347,13 +345,11 @@
         own_v[0, :, pair_cols(p)] = dot_nn(ds2[p], qb[0, p]) * scale
         own_v[1, :, pair_cols(p)] = dot_nn(p2[p], qb[1, p])
 
-    for copy in near_in:
-        copy.wait_send()
-
-    @pl.when(has_f)
-    def _():
-        for copy in (*far_in[Q], *far_in[K], *far_in[V], *far_in[C], es_f):
-            copy.wait_send()
+    for p in range(pairs):
+        kv_video[p].wait_recv()
+        for t in range(2):
+            cols = pair_cols(p)
+            out[place(3 + t), cols] = (own_v[t, :, cols] + r_video[t, :, cols].astype(F32)).astype(BF16)
 
     kv_near.wait_recv()
     for pair, copies, p in (
@@ -370,31 +366,22 @@
             if t in (DK, DV):
                 total += r_near[t, :, cols].astype(F32)
             out[place({OUT: 1, DQ: 5, DK: 6, DV: 7}[t]), cols] = total.astype(BF16)
-    for p in range(pairs):
-        kv_video[p].wait_recv()
-        for t in range(2):
-            cols = pair_cols(p)
-            out[place(3 + t), cols] = (own_v[t, :, cols] + r_video[t, :, cols].astype(F32)).astype(BF16)
-
-    for copy in (kv_near, *kv_video):
-        copy.wait_send()
-
-    @pl.when(has_f)
-    def _():
-        for copy in (*kv_far, *oq_far, ls_f):
-            copy.wait_send()
+    wait_for(out, to_n)
+
+    @pl.when(has_f)
+    def _():
+        wait_for(out.at[pl.ds(0, 8 * arows)], to_f)
+        es_f.wait_send()
+        ls_f.wait_send()
 
 
 def spread(sizes, joint, *refs):
-    outs, sems = refs[: len(sizes)], refs[len(sizes)]
-    start, copies = 0, []
+    outs, sem = refs[: len(sizes)], refs[len(sizes)]
+    start = 0
     for index, size in enumerate(sizes):
-        copies.append(pltpu.make_async_copy(joint.at[pl.ds(start, size)], outs[index], sems.at[index]))
+        pltpu.make_async_copy(joint.at[pl.ds(start, size)], outs[index], sem).start()
         start += size
-    for copy in copies:
-        copy.start()
-    for copy in copies:
-        copy.wait()
+    pltpu.make_async_copy(joint, joint, sem).wait()
 
 
 def local(video_query, video_key, video_value, video_cot, audio_query, audio_key, audio_value, audio_cot, intersection):
@@ -425,12 +412,13 @@
         *[pltpu.VMEM((2, 4, two), F32)] * 4,
         *[pltpu.VMEM((4, two), F32)] * 2,
         pltpu.VMEM((three, vrows), F32),
-        dma((9,)),
-        *[dma((4,))] * 2,
-        *[dma((4, pairs))] * 2,
-        *[dma((2,))] * 2,
-        *[dma((pairs,))] * 4,
-        *[dma((1 + pairs,))] * 2,
+        dma((5,)),
+        dma((2,)),
+        dma((2, pairs)),
+        dma((2,)),
+        *[dma((pairs,))] * 2,
+        dma((1 + pairs,)),
+        dma((4,)),
     ]
     any_space = pl.BlockSpec(memory_space=pl.ANY)
     in_hbm = pl.BlockSpec(memory_space=pltpu.HBM)
@@ -455,7 +443,7 @@
             out_shape=[jax.ShapeDtypeStruct((size, features), BF16) for size in sizes],
             in_specs=[any_space],
             out_specs=[any_space] * len(sizes),
-            scratch_shapes=[dma((len(sizes),))],
+            scratch_shapes=[dma],
             name="spread",
         )(joint)
     )

time: 20.7 us -> 20.3 us (0.981)
  Pallas kernels: 19.9 us -> 19.5 us
    pallas_call x1, Pallas kernels: 18.9 us -> 18.5 us  [local(): pl.pallas_call(functools.partial(kernel, blocks, vrows, arows, heads), ou...]
where the time goes in v4:
time: 20.3 us; the launch traced here: 20.1 us
  Pallas kernels  19.5 us (96%)
  between operations  0.64 us (3%)
    pallas_call x1, Pallas kernels, local(): pl.pallas_call(functools.partial(kernel, blocks, vrows, arows, heads), ou...  18.5 us
    pallas_call x1, Pallas kernels, local(): pl.pallas_call(functools.partial(spread, sizes), out_shape=[jax.ShapeDtyp...  1.01 us

profile of v4, /device:TPU:1, one launch (start us, length us, event | category | flops | bytes accessed | tf_op | source)
XLA Modules:
  0.0 20.1 jit_solution(13157479491039195951)
XLA Ops:
  0.6 18.5 %cross_attention.1.joint = bf16[768,768]{1,0:T(8,128)(2,1)S(1)} custom-call(bf16[128,768]{1,0:T(8,128)(2,1)} %refs_0_.1, bf16[128,768]{1,0:T(8,128)(2,1)} %refs_1_.1, bf16[128,768]{1,0:T(8,128)(2,1)} %refs_2_.1, bf16[128,768]{1,0:T(8,128)(2,1)} %refs_3_.1, bf16[64,768]{1,0:T(8,128)(2,1)} %refs_4_.1, bf16[64,768]{1,0:T(8,128)(2,1)} %refs_5_.1, ...), custom_call_target="tpu_custom_call" | custom-call | flops 452984832 | bytes 1769472 | tf_op jit(solution)/shard_map/cross_attention/pallas_call | solution.py:425
  19.1 1.0 %spread.1 = (bf16[128,768]{1,0:T(8,128)(2,1)}, bf16[64,768]{1,0:T(8,128)(2,1)}, bf16[128,768]{1,0:T(8,128)(2,1)}, bf16[128,768]{1,0:T(8,128)(2,1)}, bf16[128,768...) custom-call(bf16[768,768]{1,0:T(8,128)(2,1)S(1)} %cross_attention.1.joint), custom_call_target="tpu_custom_call" | custom-call | tf_op jit(solution)/shard_map/spread/pallas_call | solution.py:441

commit v5 on v4

--- a/solution.py
+++ b/solution.py
@@ -16,8 +16,10 @@
 BF16 = jnp.bfloat16
 Q, K, V, C = 0, 1, 2, 3
 DK, DV, OUT, DQ = 0, 1, 2, 3
-FIRST = ((K, 1), (V, 1), (Q, 0), (C, 0), (Q, 1), (C, 1))
-LATER = ((Q, 2), (C, 2), (K, 2), (V, 2))
+KV_CHUNKS = ((0, 1), (1, 3), (3, 5), (5, 6))
+QC, KV = 0, 1
+FIRST = ((KV, 1), (QC, 0),)
+LATER = ((QC, 1), (QC, 2), (KV, 2), (KV, 3),)
 
 
 def dot_nt(a, b):
@@ -43,7 +45,7 @@
     (vq, vk, vv, vc, aq, ak, av, ac, inter, out) = refs[:10]
     (spans, vqc, vkv, qc, win, qb, e_on, dp_on, e_far, dp_far, p1, ds1, p2, ds2, own_a, own_v,
      s_near, r_near, s_video, r_video, s_far, r_far, es, ls, re_f, rl_f, m_on, m_far, bias,
-     load_sem, near_sem, far_sem, terms_sem, kv_sem, oq_sem, back_sem, sent) = refs[10:]
+     load_sem, near_sem, qc_sem, far_sem, terms_sem, kv_sem, oq_sem, back_sem, sent) = refs[10:]
     scale = DH ** (-0.5)
     scale2 = scale * LOG2E
     two = 2 * arows
@@ -68,16 +70,16 @@
 
     pl.semaphore_signal(barrier, inc=1, device_id=here(n), device_id_type=MESH)
 
-    span_load = pltpu.make_async_copy(inter, spans, load_sem.at[4])
+    span_load = pltpu.make_async_copy(inter, spans, load_sem.at[1])
     loads = [
         pltpu.make_async_copy(vk, vkv.at[0, pl.ds(0, vrows)], load_sem.at[0]),
         pltpu.make_async_copy(vv, vkv.at[1, pl.ds(0, vrows)], load_sem.at[0]),
-        pltpu.make_async_copy(aq, qc.at[0, pl.ds(0, arows)], load_sem.at[1]),
-        pltpu.make_async_copy(ac, qc.at[1, pl.ds(0, arows)], load_sem.at[1]),
-        pltpu.make_async_copy(ak, win.at[0, pl.ds(0, arows)], load_sem.at[2]),
-        pltpu.make_async_copy(av, win.at[1, pl.ds(0, arows)], load_sem.at[2]),
-        pltpu.make_async_copy(vq, vqc.at[0], load_sem.at[3]),
-        pltpu.make_async_copy(vc, vqc.at[1], load_sem.at[3]),
+        pltpu.make_async_copy(aq, qc.at[0, pl.ds(0, arows)], load_sem.at[0]),
+        pltpu.make_async_copy(ac, qc.at[1, pl.ds(0, arows)], load_sem.at[0]),
+        pltpu.make_async_copy(ak, win.at[0, pl.ds(0, arows)], load_sem.at[0]),
+        pltpu.make_async_copy(av, win.at[1, pl.ds(0, arows)], load_sem.at[0]),
+        pltpu.make_async_copy(vq, vqc.at[0], load_sem.at[0]),
+        pltpu.make_async_copy(vc, vqc.at[1], load_sem.at[0]),
     ]
     for copy in (span_load, *loads):
         copy.start()
@@ -95,6 +97,9 @@
 
     def head_cols(h):
         return pl.ds(h * DH, DH)
+
+    def chunk_cols(c):
+        return pl.ds(KV_CHUNKS[c][0] * DH, (KV_CHUNKS[c][1] - KV_CHUNKS[c][0]) * DH)
 
     to_n, to_f = sent.at[0], sent.at[1]
     near_in = [
@@ -106,28 +111,29 @@
             (av, win.at[1, pl.ds(arows, arows)]),
         ))
     ]
-    far_in = [
-        [remote(ref.at[:, pair_cols(p)], dst.at[:, pair_cols(p)], to_f, far_sem.at[kind, p], f) for p in range(pairs)]
-        for ref, dst, kind in (
-            (aq, qc.at[0, pl.ds(arows, arows)], 0),
-            (ak, win.at[0, pl.ds(two, arows)], 1),
-            (av, win.at[1, pl.ds(two, arows)], 1),
-            (ac, qc.at[1, pl.ds(arows, arows)], 0),
-        )
+    far_qc = [
+        [remote(ref.at[:, pair_cols(p)], qc.at[t, pl.ds(arows, arows), pair_cols(p)], to_f, qc_sem.at[p], f)
+         for t, ref in enumerate((aq, ac))]
+        for p in range(pairs)
+    ]
+    far_kv = [
+        [remote(ref.at[:, chunk_cols(c)], win.at[t, pl.ds(two, arows), chunk_cols(c)], to_f, far_sem.at[c], f)
+         for t, ref in enumerate((ak, av))]
+        for c in range(len(KV_CHUNKS))
     ]
     es_f = remote(es, re_f, sent.at[2], terms_sem.at[0], f)
-    ls_f = remote(ls, rl_f, sent.at[3], terms_sem.at[1], f)
+    ls_f = remote(ls, rl_f, sent.at[2], terms_sem.at[1], f)
     kv_far = [
-        remote(s_far.at[pl.ds(0, 2), :, pair_cols(p)], r_far.at[pl.ds(0, 2), :, pair_cols(p)], to_f, kv_sem.at[p], f)
-        for p in range(pairs)
+        remote(s_far.at[pl.ds(0, 2), :, chunk_cols(c)], r_far.at[pl.ds(0, 2), :, chunk_cols(c)], to_f, kv_sem.at[c], f)
+        for c in range(len(KV_CHUNKS))
     ]
     oq_far = [
         remote(s_far.at[pl.ds(2, 2), :, pair_cols(p)], r_far.at[pl.ds(2, 2), :, pair_cols(p)], to_f, oq_sem.at[p], f)
         for p in range(pairs)
     ]
-    kv_near = remote(s_near, r_near, to_n, back_sem.at[pairs], n)
+    kv_near = remote(s_near, r_near, to_n, back_sem.at[0], n)
     kv_video = [
-        remote(s_video.at[:, :, pair_cols(p)], r_video.at[:, :, pair_cols(p)], to_n, back_sem.at[p], n)
+        remote(s_video.at[:, :, pair_cols(p)], r_video.at[:, :, pair_cols(p)], to_n, back_sem.at[1], n)
         for p in range(pairs)
     ]
 
@@ -144,16 +150,17 @@
 
     @pl.when(has_f)
     def _():
-        far_in[K][0].start()
-        far_in[V][0].start()
+        for copy in far_kv[0]:
+            copy.start()
 
     for copy in near_in:
         copy.start()
 
     @pl.when(has_f)
     def _():
-        for t, p in FIRST:
-            far_in[t][p].start()
+        for kind, index in FIRST:
+            for copy in (far_qc, far_kv)[kind][index]:
+                copy.start()
 
     span_load.wait()
     first, last = spans[0, b], spans[1, b]
@@ -178,10 +185,7 @@
             ref[0] = jnp.full(ref.shape[1:], NEG, F32)
             ref[1] = jnp.zeros(ref.shape[1:], F32)
 
-    wait_for(vkv.at[:, pl.ds(0, vrows)], load_sem.at[0])
-    wait_for(qc.at[:, pl.ds(0, arows)], load_sem.at[1])
-    wait_for(win.at[:, pl.ds(0, arows)], load_sem.at[2])
-    wait_for(vqc, load_sem.at[3])
+    wait_for(out, load_sem.at[0])
 
     def place_blocks(p, start):
         for t in range(2):
@@ -193,35 +197,41 @@
     for p in range(pairs):
         place_blocks(p, 0)
 
+    for p in range(pairs):
+        e_on[p, pl.ds(0, vrows), :] = dot_nt(vkv[0, pl.ds(0, vrows), pair_cols(p)], qb[0, p, pl.ds(0, two), :]) * scale2
+        dp_on[p, pl.ds(0, vrows), :] = dot_nt(vkv[1, pl.ds(0, vrows), pair_cols(p)], qb[1, p, pl.ds(0, two), :])
+
     wait_for(vkv.at[:, pl.ds(vrows, vrows)], near_sem.at[0])
-
-    for p in range(pairs):
-        s = dot_nt(vkv[0, :, pair_cols(p)], qb[0, p, pl.ds(0, two), :]) * scale2
-        dp = dot_nt(vkv[1, :, pair_cols(p)], qb[1, p, pl.ds(0, two), :])
-        s = jnp.concatenate([s[:vrows], s[vrows:] + bias_near], axis=0)
-        top = jnp.max(s, axis=0, keepdims=True)
-        e = jnp.exp2(s - top)
-        e_on[p] = e
-        dp_on[p] = dp
-        total = jnp.sum(e, axis=0, keepdims=True)
+    for p in range(pairs):
+        near = pl.ds(vrows, vrows)
+        s_own, dp_own = e_on[p, pl.ds(0, vrows), :], dp_on[p, pl.ds(0, vrows), :]
+        s = dot_nt(vkv[0, near, pair_cols(p)], qb[0, p, pl.ds(0, two), :]) * scale2 + bias_near
+        dp = dot_nt(vkv[1, near, pair_cols(p)], qb[1, p, pl.ds(0, two), :])
+        top = jnp.maximum(jnp.max(s, axis=0, keepdims=True), jnp.max(s_own, axis=0, keepdims=True))
+        e, e_own = jnp.exp2(s - top), jnp.exp2(s_own - top)
+        e_on[p, pl.ds(0, vrows), :] = e_own
+        e_on[p, near, :] = e
+        dp_on[p, near, :] = dp
+        total = jnp.sum(e + e_own, axis=0, keepdims=True)
         m_on[pl.ds(p, 1), :] = top
         es[0, pl.ds(p, 1), :] = top + jnp.log(total) * LOG2E
-        es[1, pl.ds(p, 1), :] = jnp.sum(e * dp, axis=0, keepdims=True) / total
+        es[1, pl.ds(p, 1), :] = jnp.sum(e * dp + e_own * dp_own, axis=0, keepdims=True) / total
 
     @pl.when(has_f)
     def _():
         es_f.start()
-        for t, p in LATER:
-            far_in[t][p].start()
+        for kind, index in LATER:
+            for copy in (far_qc, far_kv)[kind][index]:
+                copy.start()
 
     wait_for(win.at[:, pl.ds(arows, arows)], near_sem.at[1])
 
-    def stage_scores(p):
+    def stage_scores(c):
         @pl.when(has_f)
         def _():
-            wait_for(win.at[:, pl.ds(two, arows), pair_cols(p)], far_sem.at[1, p])
-
-        for h in (2 * p, 2 * p + 1):
+            wait_for(win.at[:, pl.ds(two, arows), chunk_cols(c)], far_sem.at[c])
+
+        for h in range(*KV_CHUNKS[c]):
             cols = head_cols(h)
             qv, cv = vqc[0, :, cols], vqc[1, :, cols]
             s = dot_nt(win[0, :, cols], qv) * scale2 + bias[...]
@@ -240,12 +250,12 @@
 
         @pl.when(has_f)
         def _():
-            kv_far[p].start()
+            kv_far[c].start()
 
     def stage_terms(p):
         @pl.when(has_f)
         def _():
-            wait_for(qc.at[:, pl.ds(arows, arows), pair_cols(p)], far_sem.at[0, p])
+            wait_for(qc.at[:, pl.ds(arows, arows), pair_cols(p)], qc_sem.at[p])
 
         place_blocks(p, arows)
         s = dot_nt(vkv[0, pl.ds(0, vrows), pair_cols(p)], qb[0, p, pl.ds(two, two), :]) * scale2
@@ -290,15 +300,16 @@
 
     stage_far(0)
     stage_terms(1)
+    stage_far(1)
     stage_terms(2)
 
     @pl.when(has_f)
     def _():
         ls_f.start()
 
-    stage_far(1)
     stage_far(2)
     stage_scores(2)
+    stage_scores(3)
 
     for h in range(heads):
         cols = head_cols(h)
@@ -345,23 +356,26 @@
         own_v[0, :, pair_cols(p)] = dot_nn(ds2[p], qb[0, p]) * scale
         own_v[1, :, pair_cols(p)] = dot_nn(p2[p], qb[1, p])
 
-    for p in range(pairs):
-        kv_video[p].wait_recv()
-        for t in range(2):
-            cols = pair_cols(p)
-            out[place(3 + t), cols] = (own_v[t, :, cols] + r_video[t, :, cols].astype(F32)).astype(BF16)
+    wait_for(r_video, back_sem.at[1])
+    for t in range(2):
+        out[place(3 + t), :] = (own_v[t] + r_video[t].astype(F32)).astype(BF16)
 
     kv_near.wait_recv()
     for pair, copies, p in (
-        ((DK, DV), kv_far, 0), ((DK, DV), kv_far, 1), ((OUT, DQ), oq_far, 0),
-        ((OUT, DQ), oq_far, 1), ((OUT, DQ), oq_far, 2), ((DK, DV), kv_far, 2),
+        ((DK, DV), kv_far, 0),
+        ((DK, DV), kv_far, 1),
+        ((OUT, DQ), oq_far, 0),
+        ((OUT, DQ), oq_far, 1),
+        ((OUT, DQ), oq_far, 2),
+        ((DK, DV), kv_far, 2),
+        ((DK, DV), kv_far, 3),
     ):
         @pl.when(has_f)
         def _(copy=copies[p]):
             copy.wait_recv()
 
         for t in pair:
-            cols = pair_cols(p)
+            cols = chunk_cols(p) if copies is kv_far else pair_cols(p)
             total = own_a[t, :, cols] + r_far[t, :, cols].astype(F32)
             if t in (DK, DV):
                 total += r_near[t, :, cols].astype(F32)
@@ -371,8 +385,7 @@
     @pl.when(has_f)
     def _():
         wait_for(out.at[pl.ds(0, 8 * arows)], to_f)
-        es_f.wait_send()
-        ls_f.wait_send()
+        wait_for(bias.at[pl.ds(0, 16)], sent.at[2])
 
 
 def spread(sizes, joint, *refs):
@@ -412,13 +425,15 @@
         *[pltpu.VMEM((2, 4, two), F32)] * 4,
         *[pltpu.VMEM((4, two), F32)] * 2,
         pltpu.VMEM((three, vrows), F32),
-        dma((5,)),
         dma((2,)),
-        dma((2, pairs)),
         dma((2,)),
-        *[dma((pairs,))] * 2,
-        dma((1 + pairs,)),
-        dma((4,)),
+        dma((pairs,)),
+        dma((len(KV_CHUNKS),)),
+        dma((2,)),
+        dma((len(KV_CHUNKS),)),
+        dma((pairs,)),
+        dma((2,)),
+        dma((3,)),
     ]
     any_space = pl.BlockSpec(memory_space=pl.ANY)
     in_hbm = pl.BlockSpec(memory_space=pltpu.HBM)

time: 20.3 us -> 19.7 us (0.970)
  Pallas kernels: 19.5 us -> 19 us
    pallas_call x1, Pallas kernels: 18.5 us -> 17.9 us  [local(): pl.pallas_call(functools.partial(kernel, blocks, vrows, arows, heads), ou...]
where the time goes in v5:
time: 19.7 us; the launch traced here: 19.6 us
  Pallas kernels  19 us (96%)
  between operations  0.64 us (3%)
    pallas_call x1, Pallas kernels, local(): pl.pallas_call(functools.partial(kernel, blocks, vrows, arows, heads), ou...  17.9 us
    pallas_call x1, Pallas kernels, local(): pl.pallas_call(functools.partial(spread, sizes), out_shape=[jax.ShapeDtyp...  1.01 us

profile of v5, /device:TPU:1, one launch (start us, length us, event | category | flops | bytes accessed | tf_op | source)
XLA Modules:
  0.0 19.6 jit_solution(15116033447142778642)
XLA Ops:
  0.6 17.9 %cross_attention.1.joint = bf16[768,768]{1,0:T(8,128)(2,1)S(1)} custom-call(bf16[128,768]{1,0:T(8,128)(2,1)} %refs_0_.1, bf16[128,768]{1,0:T(8,128)(2,1)} %refs_1_.1, bf16[128,768]{1,0:T(8,128)(2,1)} %refs_2_.1, bf16[128,768]{1,0:T(8,128)(2,1)} %refs_3_.1, bf16[64,768]{1,0:T(8,128)(2,1)} %refs_4_.1, bf16[64,768]{1,0:T(8,128)(2,1)} %refs_5_.1, ...), custom_call_target="tpu_custom_call" | custom-call | flops 452984832 | bytes 1769472 | tf_op jit(solution)/shard_map/cross_attention/pallas_call | solution.py:440
  18.6 1.0 %spread.1 = (bf16[128,768]{1,0:T(8,128)(2,1)}, bf16[64,768]{1,0:T(8,128)(2,1)}, bf16[128,768]{1,0:T(8,128)(2,1)}, bf16[128,768]{1,0:T(8,128)(2,1)}, bf16[128,768...) custom-call(bf16[768,768]{1,0:T(8,128)(2,1)S(1)} %cross_attention.1.joint), custom_call_target="tpu_custom_call" | custom-call | tf_op jit(solution)/shard_map/spread/pallas_call | solution.py:456

commit v6 on v5

--- a/solution.py
+++ b/solution.py
@@ -16,10 +16,10 @@
 BF16 = jnp.bfloat16
 Q, K, V, C = 0, 1, 2, 3
 DK, DV, OUT, DQ = 0, 1, 2, 3
-KV_CHUNKS = ((0, 1), (1, 3), (3, 5), (5, 6))
+KV_CHUNKS = ((0, 1), (1, 3), (3, 4), (4, 5), (5, 6))
 QC, KV = 0, 1
-FIRST = ((KV, 1), (QC, 0),)
-LATER = ((QC, 1), (QC, 2), (KV, 2), (KV, 3),)
+FIRST = ((KV, 1), (KV, 2), (QC, 0))
+LATER = ((QC, 1), (QC, 2), (KV, 3), (KV, 4))
 
 
 def dot_nt(a, b):
@@ -292,6 +292,7 @@
 
     stage_scores(0)
     stage_scores(1)
+    stage_scores(2)
     stage_terms(0)
 
     @pl.when(has_f)
@@ -308,8 +309,8 @@
         ls_f.start()
 
     stage_far(2)
-    stage_scores(2)
     stage_scores(3)
+    stage_scores(4)
 
     for h in range(heads):
         cols = head_cols(h)
@@ -369,6 +370,7 @@
         ((OUT, DQ), oq_far, 2),
         ((DK, DV), kv_far, 2),
         ((DK, DV), kv_far, 3),
+        ((DK, DV), kv_far, 4),
     ):
         @pl.when(has_f)
         def _(copy=copies[p]):

time: 19.7 us -> 20 us (1.015)
    pallas_call x1, Pallas kernels: 17.9 us -> 18.2 us  [local(): pl.pallas_call(functools.partial(kernel, blocks, vrows, arows, heads), ou...]
where the time goes in v6:
time: 20 us; the launch traced here: 19.8 us
  Pallas kernels  19.2 us (96%)
  between operations  0.64 us (3%)
    pallas_call x1, Pallas kernels, local(): pl.pallas_call(functools.partial(kernel, blocks, vrows, arows, heads), ou...  18.2 us
    pallas_call x1, Pallas kernels, local(): pl.pallas_call(functools.partial(spread, sizes), out_shape=[jax.ShapeDtyp...  1.01 us

profile of v6, /device:TPU:1, one launch (start us, length us, event | category | flops | bytes accessed | tf_op | source)
XLA Modules:
  0.0 19.8 jit_solution(4105997417641233349)
XLA Ops:
  0.6 18.2 %cross_attention.1.joint = bf16[768,768]{1,0:T(8,128)(2,1)S(1)} custom-call(bf16[128,768]{1,0:T(8,128)(2,1)} %refs_0_.1, bf16[128,768]{1,0:T(8,128)(2,1)} %refs_1_.1, bf16[128,768]{1,0:T(8,128)(2,1)} %refs_2_.1, bf16[128,768]{1,0:T(8,128)(2,1)} %refs_3_.1, bf16[64,768]{1,0:T(8,128)(2,1)} %refs_4_.1, bf16[64,768]{1,0:T(8,128)(2,1)} %refs_5_.1, ...), custom_call_target="tpu_custom_call" | custom-call | flops 452984832 | bytes 1769472 | tf_op jit(solution)/shard_map/cross_attention/pallas_call | solution.py:442
  18.8 1.0 %spread.1 = (bf16[128,768]{1,0:T(8,128)(2,1)}, bf16[64,768]{1,0:T(8,128)(2,1)}, bf16[128,768]{1,0:T(8,128)(2,1)}, bf16[128,768]{1,0:T(8,128)(2,1)}, bf16[128,768...) custom-call(bf16[768,768]{1,0:T(8,128)(2,1)S(1)} %cross_attention.1.joint), custom_call_target="tpu_custom_call" | custom-call | tf_op jit(solution)/shard_map/spread/pallas_call | solution.py:458
